TPU v7x, 256 devices: a whole 4x4x8 slice. The times are simulated.
256 devices in a mesh: ctx: 16 (over z, core), grp: 16 (over y, x).
Axes of the slice: x: 4, y: 4, z: 8, core: 2. Of those that a mesh axis runs over, the one named last changes fastest.
Arguments:
- queries: bfloat16 [4096, 36864], P('ctx', 'grp'), may hold values from -20 to 20
- latent_cache: bfloat16 [1024, 36864], P('ctx'), may hold values from -18 to 18
- block_picks: int32 [16, 32], P('ctx'), may hold values from 0 to 1023, as said below
- out_grad: bfloat16 [4096, 32768], P('ctx', 'grp'), may hold values from -16 to 16
Outputs:
- query_grad: bfloat16 [4096, 36864], P('ctx', 'grp')
- latent_grad: bfloat16 [1024, 36864], P(('ctx', 'grp'))
Inputs may be any that keep to these rules, and one draw needn't show every extreme that they name: `block_picks`: A row names 32 different blocks. The 1 row of one index of ctx name no block twice, and name at most 4 blocks of any one index's range of 64 blocks, exactly 4 of one such range.
All inputs are finite; a program needn't handle non-finite values.
Results may differ from a plain program's by a relative error of at most 0.023.
Values may be sent and summed in bfloat16 or wider, within the bound.
No kernel may reach another device: no remote copies, remote signals or barrier semaphores. Data moves between devices by JAX's collectives and lax.ppermute only.
A program may use at most 128 MiB of HBM per device.

v0:
```python
import jax
import jax.numpy as jnp
from jax import lax
from jax.sharding import PartitionSpec as P

DL = 512
DR = 64
BLK = 64
TOPK = 32
QBLK = 256
DK = 576


SCORE_SCALE = 192.0 ** (-0.5)


def on_device(queries, latent_cache, block_picks, out_grad):
    shards = lax.axis_size("ctx")
    block_count = latent_cache.shape[0]
    head_count = queries.shape[1] // DK
    query_rows = queries.shape[0]
    qblocks = query_rows // QBLK
    pick_total = qblocks * TOPK
    capacity = 2 * pick_total // shards
    slot_total = shards * capacity
    flat_ids = block_picks.reshape(-1)
    holder = flat_ids // block_count
    within = flat_ids % block_count
    counter = jnp.arange(pick_total, dtype=jnp.int32)
    earlier = (holder[:, None] == holder[None, :]) & (counter[None, :] < counter[:, None])
    position = holder * capacity + jnp.sum(earlier.astype(jnp.int32), axis=1)
    wanted = jnp.zeros((slot_total,), jnp.int32).at[position].set(within).reshape(shards, capacity)
    asked = lax.all_to_all(wanted, "ctx", split_axis=0, concat_axis=0, tiled=True)
    served = jnp.take(latent_cache, asked.reshape(-1), axis=0)
    fetched = lax.all_to_all(
        served.reshape(shards, capacity, BLK * DK), "ctx", split_axis=0, concat_axis=0, tiled=True
    )
    fetched = fetched.reshape(slot_total, BLK * DK)
    picked = jnp.take(fetched, position, axis=0).reshape(qblocks, TOPK * BLK, DK)
    query_blocks = queries.reshape(qblocks, QBLK, head_count, DK)
    grad_blocks = out_grad.reshape(qblocks, QBLK, head_count, DL)
    block_keys = picked[0]
    scores = (
        jnp.einsum("qhd,kd->hqk", query_blocks[0], block_keys, preferred_element_type=jnp.float32)
        * SCORE_SCALE
    )
    row_peak = jnp.max(scores, axis=2, keepdims=True)
    weights = jnp.exp(scores - row_peak)
    attention = weights / jnp.sum(weights, axis=2, keepdims=True)
    dprobs = jnp.einsum(
        "qhe,ke->hqk", grad_blocks[0], block_keys[:, :DL], preferred_element_type=jnp.float32
    )
    inner_sum = jnp.sum(attention * dprobs, axis=2, keepdims=True)
    dscores = (attention * (dprobs - inner_sum) * SCORE_SCALE).astype(jnp.bfloat16)
    probs_low = attention.astype(jnp.bfloat16)
    query_grad = jnp.einsum("hqk,kd->qhd", dscores, block_keys, preferred_element_type=jnp.float32)
    query_list = [query_grad.astype(jnp.bfloat16)]
    dscore_list = [dscores]
    probs_list = [probs_low]
    query_grads = jnp.stack(query_list).reshape(query_rows, head_count * DK)
    dscore_all = jnp.stack(dscore_list).reshape(qblocks, head_count, QBLK, TOPK, BLK)
    probs_all = jnp.stack(probs_list).reshape(qblocks, head_count, QBLK, TOPK, BLK)
    block_range = jnp.arange(block_count, dtype=jnp.int32)
    key_part = jnp.einsum(
        "bhqjr,bqhd->rbjd", dscore_all, query_blocks, preferred_element_type=jnp.float32
    )
    value_part = jnp.einsum(
        "bhqjr,bqhe->rbje", probs_all, grad_blocks, preferred_element_type=jnp.float32
    )
    value_part = jnp.pad(value_part, ((0, 0), (0, 0), (0, 0), (0, DR)))
    combined = (key_part + value_part).reshape(BLK, pick_total, DK)
    placed = jnp.zeros((BLK, slot_total, DK), jnp.float32).at[:, position, :].set(combined)
    whole = (
        placed.reshape(BLK, slot_total * DK)
        .astype(jnp.bfloat16)
        .reshape(BLK, shards, capacity * DK)
    )
    returned = lax.all_to_all(whole, "ctx", split_axis=1, concat_axis=1, tiled=True)
    returned = returned.reshape(BLK, slot_total, DK)
    one_hot = (asked.reshape(-1)[:, None] == block_range[None, :]).astype(jnp.bfloat16)
    owner_sum = jnp.einsum("rsd,sb->brd", returned, one_hot, preferred_element_type=jnp.float32)
    owner_sum = owner_sum.reshape(block_count, BLK * DK)
    latent_grad = lax.psum_scatter(
        owner_sum.astype(jnp.bfloat16), "grp", scatter_dimension=0, tiled=True
    )
    return (query_grads, latent_grad)


def solution(mesh):
    placed = (P("ctx", "grp"), P("ctx", None), P("ctx", None), P("ctx", "grp"))
    return jax.shard_map(
        on_device,
        mesh=mesh,
        in_specs=placed,
        out_specs=(P("ctx", "grp"), P(("ctx", "grp"), None)),
        check_vma=False,
    )
```

profile of v0, /device:TPU:1, one launch (start us, length us, event | category | flops | bytes accessed | tf_op | source)
XLA Modules:
  0.0 551.2 jit_solution(15356992381412625945)
XLA Ops:
  10.1 16.8 %all_to_all.19 = s32[16,1,4]{2,1,0:T(1,128)S(1)} all-to-all(s32[16,1,4]{2,1,0:T(1,128)S(1)} %bitcast.132), channel_id=1, replica_groups=mesh['ctx'=16,'grp'=16] {'ctx'}, dimensions={0} | all-to-all | bytes 512 | tf_op jit(solution)/shard_map/all_to_all | solution.py:33
  28.4 12.6 %gather_fusion = bf16[64,36864]{1,0:T(8,128)(2,1)} fusion(bf16[64,36864]{1,0:T(8,128)(2,1)} %param.5, s32[1024]{0:T(1024)S(1)} %pad_clamp_fusion.1), kind=kCustom, calls=%fused_computation | custom fusion | bytes 9437440 | tf_op jit(solution)/shard_map/jit(_take)/gather | solution.py:34
  41.0 7.6 %gather.13 = bf16[16,4,36864]{2,1,0:T(4,128)(2,1)} reshape(bf16[64,36864]{1,0:T(8,128)(2,1)} %gather_fusion) | data formatting | bytes 9437184 | tf_op jit(solution)/shard_map/jit(_take)/gather | solution.py:34
  48.6 6.6 %broadcast_select_fusion = bf16[16,4,36864]{2,1,0:T(4,128)(2,1)} fusion(bf16[16,4,36864]{2,1,0:T(4,128)(2,1)} %gather.13, pred[16,4]{1,0:T(8,128)(4,1)S(1)} %copy.59), kind=kLoop, calls=%fused_computation.19 | loop fusion | flops 2359296 | bytes 9437248 | tf_op jit(solution)/shard_map/jit(_take)/select_n | solution.py:34
  55.2 5.4 all-to-all-start.1
  63.7 101.5 %all-to-all-done.1 = bf16[16,4,36864]{2,1,0:T(4,128)(2,1)} async-done(((bf16[16,4,36864]{2,1,0:T(4,128)(2,1)}), bf16[16,4,36864]{2,1,0:T(4,128)(2,1)}, u32[]{:S(2)}, u32[]{:S(2)}) %all-to-all-start.1) | async-done | bytes 4718624 | tf_op jit(solution)/shard_map/all_to_all | solution.py:35
  165.3 7.4 %reshape.232 = bf16[64,36864]{1,0:T(8,128)(2,1)} reshape(bf16[16,4,36864]{2,1,0:T(4,128)(2,1)} %all-to-all-done.1) | data formatting | bytes 9437184 | tf_op jit(solution)/shard_map/reshape | solution.py:38
  172.6 7.0 %gather_fusion.1 = bf16[32,36864]{1,0:T(8,128)(2,1)S(1)} fusion(bf16[64,36864]{1,0:T(8,128)(2,1)} %reshape.232, s32[1024]{0:T(1024)S(1)} %pad_clamp_fusion), kind=kCustom, calls=%fused_computation.1 | custom fusion | bytes 4718720 | tf_op jit(solution)/shard_map/jit(_take)/gather | solution.py:39
  190.1 6.8 %fusion.13 = f32[2048,256,4]{1,0,2:T(8,128)} fusion(bf16[256,4,576]{0,2,1:T(8,128)(2,1)} %bitcast.126, bf16[2048,576]{1,0:T(8,128)(2,1)S(1)} %select_n.95), kind=kOutput, calls=%fused_computation.23 | convolution fusion | flops 2415919104 | bytes 11927552 | tf_op jit(solution)/shard_map/qhd,kd->hqk/dot_general | solution.py:44
  196.9 8.1 %fusion.33 = (f32[4,256]{1,0:T(4,128)S(1)}, f32[4,256,2048]{1,2,0:T(8,128)S(1)}) fusion(f32[2048,256,4]{1,0,2:T(8,128)} %fusion.13), kind=kOutput, calls=%fused_computation.73 | output fusion | flops 8390655 | bytes 16781312 | tf_op jit(solution)/shard_map/sub | solution.py:48
  207.8 5.7 %fusion.17 = f32[2048,256,4]{1,0,2:T(8,128)} fusion(bf16[2048,576]{1,0:T(8,128)(2,1)S(1)} %broadcast_select_fusion.1, bf16[32,4,8,512]{3,2,1,0:T(8,128)(2,1)S(1)} %bitcast.129), kind=kOutput, calls=%fused_computation.31 | convolution fusion | flops 2147483648 | bytes 11534336 | tf_op jit(solution)/shard_map/qhe,ke->hqk/dot_general | solution.py:50
  213.5 10.4 %fusion.4 = bf16[4,256,2048]{1,2,0:T(8,128)(2,1)} fusion(f32[2048,256,4]{1,0,2:T(8,128)} %fusion.17, f32[4,256,2048]{1,2,0:T(8,128)S(1)} %get-tuple-element.15, f32[4,256]{1,0:T(4,128)S(1)} %get-tuple-element.14), kind=kOutput, calls=%fused_computation.11 | output fusion | flops 14683135 | bytes 20975616 | tf_op jit(solution)/shard_map/sub | solution.py:54
  236.9 9.7 %scatter_fusion = f32[64,64,576]{2,0,1:T(8,128)} fusion(f32[64,64,576]{2,0,1:T(8,128)} %broadcast_in_dim.59, s32[32]{0:T(128)S(1)} %fusion.26, f32[32,64,576]{2,1,0:T(8,128)} %fusion.10), kind=kCustom, calls=%fused_computation.3 | custom fusion | bytes 14155904 | tf_op jit(solution)/shard_map/scatter | solution.py:72
  256.8 9.8 %convert_element_type.34 = bf16[64,16,2304]{2,1,0:T(8,128)(2,1)} reshape(bf16[64,64,576]{2,1,0:T(8,128)(2,1)} %copy.66) | data formatting | bytes 9437184 | tf_op jit(solution)/shard_map/convert_element_type | solution.py:75
  266.5 6.0 %copy.67 = bf16[64,16,2304]{2,0,1:T(8,128)(2,1)} copy(bf16[64,16,2304]{2,1,0:T(8,128)(2,1)} %convert_element_type.34) | data formatting | bytes 9437184 | tf_op jit(solution)/shard_map/convert_element_type | solution.py:75
  272.5 5.5 %all-to-all-start.2 = ((bf16[64,16,2304]{2,0,1:T(8,128)(2,1)}), bf16[64,16,2304]{2,0,1:T(8,128)(2,1)}, u32[]{:S(2)}, u32[]{:S(2)}) async-start(bf16[64,16,2304]{2,0,1:T(8,128)(2,1)} %copy.67), calls=%async_computation.2 | async-start | bytes 9437184 | tf_op jit(solution)/shard_map/all_to_all | solution.py:78
  278.2 104.7 %all-to-all-done.2 = bf16[64,16,2304]{2,0,1:T(8,128)(2,1)} async-done(((bf16[64,16,2304]{2,0,1:T(8,128)(2,1)}), bf16[64,16,2304]{2,0,1:T(8,128)(2,1)}, u32[]{:S(2)}, u32[]{:S(2)}) %all-to-all-start.2) | async-done | bytes 4718624 | tf_op jit(solution)/shard_map/all_to_all | solution.py:78
  382.9 7.1 %copy.68 = bf16[64,16,2304]{2,1,0:T(8,128)(2,1)} copy(bf16[64,16,2304]{2,0,1:T(8,128)(2,1)} %all-to-all-done.2) | data formatting | bytes 9437184 | tf_op jit(solution)/shard_map/all_to_all | solution.py:78
  390.0 10.6 %reshape.237 = bf16[64,64,576]{2,1,0:T(8,128)(2,1)} reshape(bf16[64,16,2304]{2,1,0:T(8,128)(2,1)} %copy.68) | data formatting | bytes 9437184 | tf_op jit(solution)/shard_map/reshape | solution.py:79
  400.6 7.8 %copy.69 = bf16[64,576,64]{1,0,2:T(8,128)(2,1)} copy(bf16[64,576,64]{1,2,0:T(8,128)(2,1)} %bitcast.124) | data formatting | bytes 9437184 | tf_op jit(solution)/shard_map/rsd,sb->brd/dot_general | solution.py:81
  408.5 9.9 %dot_general.40 = bf16[36864,64]{0,1:T(8,128)(2,1)} reshape(bf16[64,576,64]{1,0,2:T(8,128)(2,1)} %copy.69) | data formatting | bytes 9437184 | tf_op jit(solution)/shard_map/rsd,sb->brd/dot_general | solution.py:81
  418.4 6.0 %convolution_convert_fusion = bf16[64,36864]{1,0:T(8,128)(2,1)} fusion(bf16[36864,64]{0,1:T(8,128)(2,1)} %dot_general.40, s32[64]{0:T(128)S(1)} %reshape.233), kind=kOutput, calls=%fused_computation.6 | convolution fusion | flops 304353280 | bytes 9437440 | tf_op jit(solution)/shard_map/rsd,sb->brd/dot_general | solution.py:81
  426.3 5.8 %fusion.18 = bf16[576,4,256]{2,0,1:T(8,128)(2,1)} fusion(bf16[4,256,2048]{1,2,0:T(8,128)(2,1)} %fusion.4, bf16[2048,576]{1,0:T(8,128)(2,1)S(1)} %copy-done.2), kind=kOutput, calls=%fused_computation.32 | convolution fusion | flops 2416508928 | bytes 7733248 | tf_op jit(solution)/shard_map/hqk,kd->qhd/dot_general | solution.py:56
  434.5 107.7 %all-reduce.4.cloned.1.call-done = bf16[64,36864]{1,0:T(8,128)(2,1)} async-done(((bf16[64,36864]{1,0:T(8,128)(2,1)}), bf16[64,36864]{1,0:T(8,128)(2,1)}) %all-reduce.4.cloned.1.call-update) | async-done | bytes 4718608
  (56 shorter events, 49.6 us)
Async XLA Ops:
  55.2 5.6 %copy-start.5 = (bf16[256,2048]{1,0:T(8,128)(2,1)S(1)}, bf16[256,2048]{1,0:T(8,128)(2,1)}, u32[]{:S(2)}) copy-start(bf16[256,2048]{1,0:T(8,128)(2,1)} %param.7) | copy-start | bytes 3145732
  55.2 7.2 %copy-start.3 = (bf16[256,2304]{1,0:T(8,128)(2,1)S(1)}, bf16[256,2304]{1,0:T(8,128)(2,1)}, u32[]{:S(2)}) copy-start(bf16[256,2304]{1,0:T(8,128)(2,1)} %param.4) | copy-start | bytes 3538948
  55.2 110.1 %all-to-all-start.1 = ((bf16[16,4,36864]{2,1,0:T(4,128)(2,1)}), bf16[16,4,36864]{2,1,0:T(4,128)(2,1)}, u32[]{:S(2)}, u32[]{:S(2)}) async-start(bf16[16,4,36864]{2,1,0:T(4,128)(2,1)} %broadcast_select_fusion), calls=%async_computation.1 | async-start | bytes 9437184 | tf_op jit(solution)/shard_map/all_to_all | solution.py:35
  196.9 8.1 %copy-start = (bf16[2048,576]{1,0:T(8,128)(2,1)S(1)}, bf16[2048,576]{1,0:T(8,128)(2,1)}, u32[]{:S(2)}) copy-start(bf16[2048,576]{1,0:T(8,128)(2,1)} %gather.15) | copy-start | bytes 7077892
  205.8 1.7 copy-start.1
  205.8 2.0 copy-start.6
  213.5 10.4 %copy-start.7 = (bf16[256,4,512]{2,1,0:T(4,128)(2,1)S(1)}, bf16[256,4,512]{2,1,0:T(4,128)(2,1)}, u32[]{:S(2)}) copy-start(bf16[256,4,512]{2,1,0:T(4,128)(2,1)} %squeeze_reshape.8) | copy-start | bytes 3145732
  223.9 2.4 copy-start.4
  223.9 2.5 copy-start.8
  272.5 110.4 %all-to-all-start.2 = ((bf16[64,16,2304]{2,0,1:T(8,128)(2,1)}), bf16[64,16,2304]{2,0,1:T(8,128)(2,1)}, u32[]{:S(2)}, u32[]{:S(2)}) async-start(bf16[64,16,2304]{2,0,1:T(8,128)(2,1)} %copy.67), calls=%async_computation.2 | async-start | bytes 9437184 | tf_op jit(solution)/shard_map/all_to_all | solution.py:78
  278.0 264.1 %all-reduce.4.cloned.1.call-start = ((), (), s32[]{:S(2)}) async-start(), calls=%async_computation.3 | async-start | bytes 9437184
  424.4 0.7 copy-start.9
  424.4 1.9 copy-start.2
Sparse Core Ops, SparseCore 0:
  424.5 117.6 all-reduce.3
where the time goes:
time: 561 us; the launch traced here: 551 us
  waiting for transfers between devices  314 us (56%)
  local copies, waits for them, and re-layouts  127 us (23%)
  other arithmetic  36 us (6%)
  matrix products  31.8 us (6%)
  blocking collectives  16.8 us (3%)
  between operations  15 us (3%)
  starting transfers between devices  11 us (2%)
    unnamed x2, waiting for transfers between devices  108 us
    all_to_all x1, waiting for transfers between devices, on_device(): lax.all_to_all(whole, 'ctx', split_axis=1, concat_axis=1, tiled=True)  105 us
    all_to_all x1, waiting for transfers between devices, on_device(): lax.all_to_all(served.reshape(shards, capacity, BLK * DK), 'ctx', split_a...  102 us
    convert_element_type x3, local copies, waits for them, and re-layouts, on_device(): whole = placed.reshape(BLK, slot_total * DK).astype(jnp.bfloat16).reshape...  21.1 us
    gather x2, local copies, waits for them, and re-layouts, on_device(): served = jnp.take(latent_cache, asked.reshape(-1), axis=0)  20.2 us
    dot_general x2, local copies, waits for them, and re-layouts, on_device(): jnp.einsum('rsd,sb->brd', returned, one_hot, preferred_element_type=jnp.f...  17.8 us
    all_to_all x1, blocking collectives, on_device(): lax.all_to_all(wanted, 'ctx', split_axis=0, concat_axis=0, tiled=True)  16.8 us
  transfers between devices with their start and end apart: 3, of which 3 were waited for; matrix products, arithmetic and copies ran while one was open for 2% of the time, Pallas kernels for 0%

commit v1 on v0

v1 whole, which is shorter than its diff:
```python
import functools
import jax
import jax.numpy as jnp
from jax import lax
from jax.experimental import pallas as pl
from jax.experimental.pallas import tpu as pltpu
from jax.sharding import PartitionSpec as P

DL = 512
DR = 64
QBLK = 256
DK = 576
SCORE_SCALE = 192.0 ** (-0.5)
LOG2E = 1.4426950408889634
F32 = jnp.float32
BF16 = jnp.bfloat16
NT = (((1,), (1,)), ((), ()))
NN = (((1,), (0,)), ((), ()))
TN = (((0,), (0,)), ((), ()))


def attend_kernel(heads, reps, x_ref, q_ref, g_ref, dq_ref, part_ref,
                  kbuf, ktbuf, qbuf, gbuf, sbuf, dpbuf, dsbuf, pbuf):
    rows = x_ref.shape[0]
    keys = rows * reps
    for r in range(reps):
        piece = x_ref[:, r * DK:(r + 1) * DK]
        kbuf[r * rows:(r + 1) * rows, :] = piece
        ktbuf[:, r * rows:(r + 1) * rows] = piece.T
    for h in range(heads):
        qbuf[h * QBLK:(h + 1) * QBLK, :] = q_ref[:, h * DK:(h + 1) * DK]
        gbuf[h * QBLK:(h + 1) * QBLK, :] = g_ref[:, h * DL:(h + 1) * DL]
    kc = 512
    nc = keys // kc

    def products(h):
        slot = h % 2
        qh = qbuf[h * QBLK:(h + 1) * QBLK, :]
        gh = gbuf[h * QBLK:(h + 1) * QBLK, :]
        for c in range(nc):
            k = kbuf[c * kc:(c + 1) * kc, :]
            sbuf[slot, c * kc:(c + 1) * kc, :] = lax.dot_general(k, qh, NT, preferred_element_type=F32)
            dpbuf[slot, c * kc:(c + 1) * kc, :] = lax.dot_general(k[:, :DL], gh, NT, preferred_element_type=F32)

    def soften(h):
        slot = h % 2
        m = jnp.max(sbuf[slot], axis=0, keepdims=True)
        factor = SCORE_SCALE * LOG2E
        total = jnp.zeros((1, QBLK), F32)
        inner = jnp.zeros((1, QBLK), F32)
        for c in range(nc):
            p = jnp.exp2((sbuf[slot, c * kc:(c + 1) * kc, :] - m) * factor)
            sbuf[slot, c * kc:(c + 1) * kc, :] = p
            total += jnp.sum(p, axis=0, keepdims=True)
            inner += jnp.sum(p * dpbuf[slot, c * kc:(c + 1) * kc, :], axis=0, keepdims=True)
        inv = 1.0 / total
        inner = inner * inv
        for c in range(nc):
            a = sbuf[slot, c * kc:(c + 1) * kc, :] * inv
            d = a * (dpbuf[slot, c * kc:(c + 1) * kc, :] - inner) * SCORE_SCALE
            pbuf[c * kc:(c + 1) * kc, h * QBLK:(h + 1) * QBLK] = a.astype(BF16)
            dsbuf[c * kc:(c + 1) * kc, h * QBLK:(h + 1) * QBLK] = d.astype(BF16)

    products(0)
    for h in range(heads):
        if h + 1 < heads:
            products(h + 1)
        soften(h)
    for r in range(reps):
        ds = dsbuf[r * rows:(r + 1) * rows, :]
        p = pbuf[r * rows:(r + 1) * rows, :]
        kp = lax.dot_general(ds, qbuf[...], NN, preferred_element_type=F32)
        vp = lax.dot_general(p, gbuf[...], NN, preferred_element_type=F32)
        part_ref[:, r * DK:r * DK + DL] = (kp[:, :DL] + vp).astype(BF16)
        part_ref[:, r * DK + DL:(r + 1) * DK] = kp[:, DL:].astype(BF16)
    for h in range(heads):
        dqt = lax.dot_general(ktbuf[...], dsbuf[:, h * QBLK:(h + 1) * QBLK], NN, preferred_element_type=F32)
        dq_ref[:, h * DK:(h + 1) * DK] = dqt.T.astype(BF16)


def attend(x, q, g):
    rows = x.shape[0]
    reps = x.shape[1] // DK
    heads = q.shape[1] // DK
    keys = rows * reps
    vm = pl.BlockSpec(memory_space=pltpu.VMEM)
    return pl.pallas_call(
        functools.partial(attend_kernel, heads, reps),
        out_shape=(jax.ShapeDtypeStruct(q.shape, BF16), jax.ShapeDtypeStruct(x.shape, BF16)),
        in_specs=[vm] * 3,
        out_specs=(vm, vm),
        scratch_shapes=[
            pltpu.VMEM((keys, DK), BF16),
            pltpu.VMEM((DK, keys), BF16),
            pltpu.VMEM((heads * QBLK, DK), BF16),
            pltpu.VMEM((heads * QBLK, DL), BF16),
            pltpu.VMEM((2, keys, QBLK), F32),
            pltpu.VMEM((2, keys, QBLK), F32),
            pltpu.VMEM((keys, heads * QBLK), BF16),
            pltpu.VMEM((keys, heads * QBLK), BF16),
        ],
        compiler_params=pltpu.CompilerParams(vmem_limit_bytes=56 * 1024 * 1024),
        name="attend",
    )(x, q, g)


def serve_kernel(place, picks_ref, cache_ref, out_ref, sums_ref):
    shards, capacity, width = out_ref.shape
    blocks = cache_ref.shape[0]
    slots = shards * capacity
    total = picks_ref.shape[1]
    per = total // shards
    picks = picks_ref[...]
    mine = (picks // blocks) == place[0]
    within = picks % blocks
    first = lax.broadcasted_iota(jnp.int32, (total, total), 0)
    second = lax.broadcasted_iota(jnp.int32, (total, total), 1)
    before = ((first // per == second // per) & (first < second)).astype(BF16)
    marks = jnp.broadcast_to(mine.astype(F32), (8, total)).astype(BF16)
    rank = lax.dot_general(marks, before, NN, preferred_element_type=F32)[:1].astype(jnp.int32)
    slot = lax.broadcasted_iota(jnp.int32, (slots, total), 0)
    asker = lax.broadcasted_iota(jnp.int32, (slots, total), 1) // per
    spot = jnp.where(mine, rank, capacity)
    left = ((slot // capacity == asker) & (slot % capacity == spot)).astype(BF16)
    block = lax.broadcasted_iota(jnp.int32, (blocks, total), 0)
    right = (block == within).astype(BF16)
    chosen = lax.dot_general(left, right, NT, preferred_element_type=F32).astype(BF16)
    sums_ref[...] = lax.dot_general(right, left, NT, preferred_element_type=F32).astype(BF16)
    served = lax.dot_general(chosen, cache_ref[...], NN, preferred_element_type=F32).astype(BF16)
    for c in range(shards):
        out_ref[c] = served[c * capacity:(c + 1) * capacity]


def serve(place, picks, cache, shards, groups):
    blocks, whole = cache.shape
    width = whole // groups
    per = picks.shape[1] // shards
    capacity = 2 * per // shards
    return pl.pallas_call(
        serve_kernel,
        out_shape=(
            jax.ShapeDtypeStruct((shards, capacity, width), BF16),
            jax.ShapeDtypeStruct((blocks, shards * capacity), BF16),
        ),
        grid_spec=pltpu.PrefetchScalarGridSpec(
            num_scalar_prefetch=1,
            grid=(1,),
            in_specs=[
                pl.BlockSpec(picks.shape, lambda i, place: (0, 0)),
                pl.BlockSpec((blocks, width), lambda i, place: (0, place[1])),
            ],
            out_specs=(
                pl.BlockSpec((shards, capacity, width), lambda i, place: (0, 0, 0)),
                pl.BlockSpec((blocks, shards * capacity), lambda i, place: (0, 0)),
            ),
        ),
        name="serve",
    )(place, picks, cache)


def compact_kernel(block_count, copies, picks_ref, recv_ref, out_ref, spot_ref):
    shards, capacity, width = recv_ref.shape
    slots = shards * capacity
    per = picks_ref.shape[1]
    picks = picks_ref[...]
    holder = picks // block_count
    first = lax.broadcasted_iota(jnp.int32, (per, per), 0)
    second = lax.broadcasted_iota(jnp.int32, (per, per), 1)
    shard = lax.broadcasted_iota(jnp.int32, (shards, per), 0)
    held = shard == holder
    before = (first < second).astype(BF16)
    counts = lax.dot_general(held.astype(BF16), before, NN, preferred_element_type=F32)
    rank = jnp.sum(jnp.where(held, counts, 0.0), axis=0, keepdims=True).astype(jnp.int32)
    slot = lax.broadcasted_iota(jnp.int32, (slots, per), 0)
    spots = (slot == holder * capacity + rank).astype(BF16)
    spot_ref[...] = spots
    recv = jnp.concatenate([recv_ref[c] for c in range(shards)], axis=0)
    picked = lax.dot_general(spots, recv, TN, preferred_element_type=F32).astype(BF16)
    for e in range(copies):
        out_ref[e * per:(e + 1) * per, :] = picked


def compact(picks, recv, block_count, copies):
    per = picks.shape[1]
    shards, capacity, width = recv.shape
    vm = pl.BlockSpec(memory_space=pltpu.VMEM)
    return pl.pallas_call(
        functools.partial(compact_kernel, block_count, copies),
        out_shape=(
            jax.ShapeDtypeStruct((copies * per, width), BF16),
            jax.ShapeDtypeStruct((shards * capacity, per), BF16),
        ),
        in_specs=[vm, vm],
        out_specs=(vm, vm),
        compiler_params=pltpu.CompilerParams(vmem_limit_bytes=32 * 1024 * 1024),
        name="compact",
    )(picks, recv)


def fold_kernel(part_ref, spot_ref, out_ref):
    shards, capacity, width = out_ref.shape
    per = spot_ref.shape[1]
    total = part_ref[:per, :].astype(F32)
    for e in range(1, part_ref.shape[0] // per):
        total += part_ref[e * per:(e + 1) * per, :].astype(F32)
    placed = lax.dot_general(
        spot_ref[...], total.astype(BF16), NN, preferred_element_type=F32
    ).astype(BF16)
    for c in range(shards):
        out_ref[c] = placed[c * capacity:(c + 1) * capacity]


def fold(parts, spots, shards):
    width = parts.shape[1]
    vm = pl.BlockSpec(memory_space=pltpu.VMEM)
    return pl.pallas_call(
        fold_kernel,
        out_shape=jax.ShapeDtypeStruct((shards, spots.shape[0] // shards, width), BF16),
        in_specs=[vm, vm],
        out_specs=vm,
        compiler_params=pltpu.CompilerParams(vmem_limit_bytes=32 * 1024 * 1024),
        name="fold",
    )(parts, spots)


def collect_kernel(recv_ref, sums_ref, out_ref):
    recv = jnp.concatenate([recv_ref[c] for c in range(recv_ref.shape[0])], axis=0)
    total = lax.dot_general(sums_ref[...], recv, NN, preferred_element_type=F32).astype(BF16)
    for e in range(out_ref.shape[0]):
        size = out_ref.shape[1]
        out_ref[e] = total[e * size:(e + 1) * size]


def collect(recv, sums, groups):
    width = recv.shape[2]
    vm = pl.BlockSpec(memory_space=pltpu.VMEM)
    return pl.pallas_call(
        collect_kernel,
        out_shape=jax.ShapeDtypeStruct((groups, sums.shape[0] // groups, width), BF16),
        in_specs=[vm, vm],
        out_specs=vm,
        compiler_params=pltpu.CompilerParams(vmem_limit_bytes=32 * 1024 * 1024),
        name="collect",
    )(recv, sums)


def on_device(queries, latent_cache, block_picks, out_grad):
    shards = lax.axis_size("ctx")
    groups = lax.axis_size("grp")
    block_count = latent_cache.shape[0]
    place = jnp.stack([lax.axis_index("ctx"), lax.axis_index("grp")]).astype(jnp.int32)
    every = lax.all_gather(block_picks, "ctx", axis=1, tiled=True)
    served, sums = serve(place, every, latent_cache, shards, groups)
    fetched = lax.all_to_all(served, "ctx", split_axis=0, concat_axis=0, tiled=True)
    picked, spots = compact(block_picks, fetched, block_count, groups)
    keys = lax.all_to_all(picked, "grp", split_axis=0, concat_axis=0, tiled=True)
    query_grad, partial = attend(keys, queries, out_grad)
    parts = lax.all_to_all(partial, "grp", split_axis=0, concat_axis=0, tiled=True)
    placed = fold(parts, spots, shards)
    returned = lax.all_to_all(placed, "ctx", split_axis=0, concat_axis=0, tiled=True)
    owned = collect(returned, sums, groups)
    final = lax.all_to_all(owned, "grp", split_axis=0, concat_axis=0, tiled=True)
    latent_grad = jnp.swapaxes(final, 0, 1).reshape(block_count // groups, latent_cache.shape[1])
    return (query_grad, latent_grad)


def solution(mesh):
    placed = (P("ctx", "grp"), P("ctx", None), P("ctx", None), P("ctx", "grp"))
    return jax.shard_map(
        on_device,
        mesh=mesh,
        in_specs=placed,
        out_specs=(P("ctx", "grp"), P(("ctx", "grp"), None)),
        check_vma=False,
    )
```

time: 561 us -> 166 us (0.30); the launches traced: 551 us -> 166 us
  waiting for transfers between devices: 314 us -> 0 us
  local copies, waits for them, and re-layouts: 127 us -> 2.74 us
  blocking collectives: 16.8 us -> 136 us
  other arithmetic: 36 us -> 0.65 us
  matrix products: 31.8 us -> 0 us
  Pallas kernels: 0 us -> 24.6 us
  between operations: 15 us -> 1.32 us
  starting transfers between devices: 11 us -> 0 us
    all_to_all x2 -> x0, waiting for transfers between devices: 206 us -> none  [the longest x1 105 us: on_device(): lax.all_to_all(whole, 'ctx', split_axis=1, concat_axis=1, tiled=True)]
    unnamed x2 -> x0, waiting for transfers between devices: 108 us -> none
    all_to_all x1 -> x5, blocking collectives: 16.8 us -> 121 us  [the longest x1 39.3 us: on_device(): lax.all_to_all(picked, 'grp', split_axis=0, concat_axis=0, tiled=True)]
    dot_general x6 -> x0, matrix products: 31.8 us -> none  [the longest x1 6.83 us: on_device(): jnp.einsum('qhd,kd->hqk', query_blocks[0], block_keys, preferred_element_...]
    gather x4 -> x0, local copies, waits for them, and re-layouts: 31.4 us -> none  [the longest x2 20.2 us: on_device(): served = jnp.take(latent_cache, asked.reshape(-1), axis=0)]
    pallas_call x0 -> x5, Pallas kernels: none -> 24.6 us  [the longest x1 20.2 us: attend(): pl.pallas_call(functools.partial(attend_kernel, heads, reps), out_shape=(...]
    convert_element_type x3 -> x0, local copies, waits for them, and re-layouts: 21.1 us -> none  [on_device(): whole = placed.reshape(BLK, slot_total * DK).astype(jnp.bfloat16).reshape...]
    sub x2 -> x0, other arithmetic: 18.5 us -> none  [the longest x1 10.4 us: on_device(): dprobs - inner_sum]
  transfers between devices with their start and end apart: 3 -> 0, of which waited for: 3 -> 0; matrix products, arithmetic and copies ran while one was open for 2% -> 0% of each run, Pallas kernels for 0% -> 0%
where the time goes in v1:
time: 166 us
  blocking collectives  136 us (82%)
  Pallas kernels  24.6 us (15%)
  local copies, waits for them, and re-layouts  2.74 us (2%)
    all_to_all x1, blocking collectives, on_device(): lax.all_to_all(picked, 'grp', split_axis=0, concat_axis=0, tiled=True)  39.3 us
    all_to_all x1, blocking collectives, on_device(): lax.all_to_all(partial, 'grp', split_axis=0, concat_axis=0, tiled=True)  34.5 us
    pallas_call x1, Pallas kernels, attend(): pl.pallas_call(functools.partial(attend_kernel, heads, reps), out_shape=(...  20.2 us
    all_to_all x1, blocking collectives, on_device(): lax.all_to_all(served, 'ctx', split_axis=0, concat_axis=0, tiled=True)  18.9 us
    all_to_all x1, blocking collectives, on_device(): lax.all_to_all(placed, 'ctx', split_axis=0, concat_axis=0, tiled=True)  16.2 us
    unnamed x1, blocking collectives  15.3 us
    all_to_all x1, blocking collectives, on_device(): lax.all_to_all(owned, 'grp', split_axis=0, concat_axis=0, tiled=True)  12.1 us

profile of v1, /device:TPU:1, one launch (start us, length us, event | category | flops | bytes accessed | tf_op | source)
XLA Modules:
  0.0 165.5 jit_solution(6473948228184779428)
XLA Ops:
  0.6 1.3 dynamic-slice
  2.6 0.8 bitcast_dynamic-update-slice_fusion
  3.3 15.3 %all-reduce = s32[512]{0:T(512)} all-reduce(s32[512]{0:T(512)S(1)} %bitcast_dynamic-update-slice_fusion), channel_id=1, replica_groups=mesh['ctx'=16,'grp'=16] {'ctx'}, use_global_device_ids=true, to_apply=%add | all-reduce | flops 512 | bytes 4096
  18.6 0.6 pad_add_fusion.place
  19.2 0.0 copy-start.1
  19.2 3.0 %serve.1 = (bf16[16,4,2304]{2,1,0:T(4,128)(2,1)}, bf16[64,64]{1,0:T(8,128)(2,1)}) custom-call(s32[2]{0:T(128)} %pad_add_fusion.place, s32[1,512]{1,0:T(1,128)} %bitcast.18, bf16[64,36864]{1,0:T(8,128)(2,1)} %cache_ref.1), custom_call_target="tpu_custom_call" | custom-call | tf_op jit(solution)/shard_map/serve/pallas_call | solution.py:139
  22.3 18.9 %all_to_all.37.recv_ref = bf16[16,4,2304]{2,1,0:T(4,128)(2,1)S(1)} all-to-all(bf16[16,4,2304]{2,1,0:T(4,128)(2,1)} %get-tuple-element.8), channel_id=1, replica_groups=mesh['ctx'=16,'grp'=16] {'ctx'}, dimensions={0} | all-to-all | bytes 589824 | tf_op jit(solution)/shard_map/all_to_all | solution.py:254
  41.1 0.0 copy-done.1
  41.1 0.6 compact.1
  41.7 39.3 %all_to_all.38 = bf16[16,32,2304]{2,1,0:T(8,128)(2,1)} all-to-all(bf16[16,32,2304]{2,1,0:T(8,128)(2,1)S(1)} %bitcast.14), channel_id=1, replica_groups=mesh['ctx'=16,'grp'=16] {'grp'}, dimensions={0} | all-to-all | bytes 4718592 | tf_op jit(solution)/shard_map/all_to_all | solution.py:256
  81.0 20.2 %attend.1 = (bf16[256,2304]{1,0:T(8,128)(2,1)}, bf16[512,2304]{1,0:T(8,128)(2,1)}) custom-call(bf16[512,2304]{1,0:T(8,128)(2,1)} %bitcast.15, bf16[256,2304]{1,0:T(8,128)(2,1)} %q_ref.1, bf16[256,2048]{1,0:T(8,128)(2,1)} %g_ref.1), custom_call_target="tpu_custom_call" | custom-call | tf_op jit(solution)/shard_map/attend/pallas_call | solution.py:87
  101.2 34.5 %all_to_all.39 = bf16[16,32,2304]{2,1,0:T(8,128)(2,1)S(1)} all-to-all(bf16[16,32,2304]{2,1,0:T(8,128)(2,1)} %bitcast.16), channel_id=1, replica_groups=mesh['ctx'=16,'grp'=16] {'grp'}, dimensions={0} | all-to-all | bytes 4718592 | tf_op jit(solution)/shard_map/all_to_all | solution.py:258
  135.7 0.0 copy-start
  135.7 0.5 fold.1
  136.2 16.2 %all_to_all.40.recv_ref = bf16[16,4,2304]{2,1,0:T(4,128)(2,1)S(1)} all-to-all(bf16[16,4,2304]{2,1,0:T(4,128)(2,1)S(1)} %fold.1), channel_id=1, replica_groups=mesh['ctx'=16,'grp'=16] {'ctx'}, dimensions={0} | all-to-all | bytes 589824 | tf_op jit(solution)/shard_map/all_to_all | solution.py:260
  152.5 0.0 copy-done
  152.5 0.2 collect.1
  152.7 12.1 %all_to_all.41 = bf16[16,4,2304]{2,1,0:T(4,128)(2,1)S(1)} all-to-all(bf16[16,4,2304]{2,1,0:T(4,128)(2,1)S(1)} %collect.1), channel_id=1, replica_groups=mesh['ctx'=16,'grp'=16] {'grp'}, dimensions={0} | all-to-all | bytes 589824 | tf_op jit(solution)/shard_map/all_to_all | solution.py:262
  164.8 0.7 copy.8
  (1 shorter events, 0.0 us)
Async XLA Ops:
  19.2 21.9 %copy-start.1 = (s32[1,32]{1,0:T(1,128)S(1)}, s32[1,32]{1,0:T(1,128)}, u32[]{:S(2)}) copy-start(s32[1,32]{1,0:T(1,128)} %picks_ref.1) | copy-start | bytes 388
  135.7 16.8 %copy-start = (bf16[64,64]{1,0:T(8,128)(2,1)S(1)}, bf16[64,64]{1,0:T(8,128)(2,1)}, u32[]{:S(2)}) copy-start(bf16[64,64]{1,0:T(8,128)(2,1)} %get-tuple-element.13.sums_ref) | copy-start | bytes 24580

commit v2 on v1

v2 whole, which is shorter than its diff:
```python
import functools
import jax
import jax.numpy as jnp
from jax import lax
from jax.experimental import pallas as pl
from jax.experimental.pallas import tpu as pltpu
from jax.sharding import PartitionSpec as P

DL = 512
DR = 64
QBLK = 256
DK = 576
SCORE_SCALE = 192.0 ** (-0.5)
LOG2E = 1.4426950408889634
F32 = jnp.float32
BF16 = jnp.bfloat16
NT = (((1,), (1,)), ((), ()))
NN = (((1,), (0,)), ((), ()))
TN = (((0,), (0,)), ((), ()))


def scores_kernel(heads, reps, near_ref, far_ref, q_ref, g_ref, ds_ref, p_ref, far_out, qbuf, gbuf,
                  kbuf, sbuf, dpbuf):
    rows = near_ref.shape[0]
    keys = 2 * rows * reps
    for half, ref in enumerate((near_ref, far_ref)):
        for r in range(reps):
            at = (half * reps + r) * rows
            kbuf[at:at + rows, :] = ref[:, r * DK:(r + 1) * DK]
    for h in range(heads):
        qbuf[h * QBLK:(h + 1) * QBLK, :] = q_ref[:, h * DK:(h + 1) * DK]
        gbuf[h * QBLK:(h + 1) * QBLK, :] = g_ref[:, h * DL:(h + 1) * DL]
    kc = 512
    nc = keys // kc
    factor = SCORE_SCALE * LOG2E

    def products(h, c, peak):
        slot = h % 2
        qh = qbuf[h * QBLK:(h + 1) * QBLK, :]
        gh = gbuf[h * QBLK:(h + 1) * QBLK, :]
        k = kbuf[c * kc:(c + 1) * kc, :]
        s = lax.dot_general(k, qh, NT, preferred_element_type=F32)
        sbuf[slot, c * kc:(c + 1) * kc, :] = s
        dpbuf[slot, c * kc:(c + 1) * kc, :] = lax.dot_general(k[:, :DL], gh, NT, preferred_element_type=F32)
        top = jnp.max(s.reshape(kc // 8, 8, QBLK), axis=0)
        return top if peak is None else jnp.maximum(peak, top)

    def weigh(h, c, m, total, inner):
        slot = h % 2
        p = jnp.exp2((sbuf[slot, c * kc:(c + 1) * kc, :] - m) * factor)
        sbuf[slot, c * kc:(c + 1) * kc, :] = p
        d = p * dpbuf[slot, c * kc:(c + 1) * kc, :]
        total += jnp.sum(p.reshape(kc // 8, 8, QBLK), axis=0)
        inner += jnp.sum(d.reshape(kc // 8, 8, QBLK), axis=0)
        return total, inner

    def finish(h, c, inv, inner):
        slot = h % 2
        a = sbuf[slot, c * kc:(c + 1) * kc, :] * inv
        d = a * ((dpbuf[slot, c * kc:(c + 1) * kc, :] - inner) * SCORE_SCALE)
        p_ref[c * kc:(c + 1) * kc, h * QBLK:(h + 1) * QBLK] = a.astype(BF16)
        ds_ref[c * kc:(c + 1) * kc, h * QBLK:(h + 1) * QBLK] = d.astype(BF16)

    peak = None
    for c in range(nc):
        peak = products(0, c, peak)
    for h in range(heads):
        m = jnp.max(peak, axis=0, keepdims=True)
        total = jnp.zeros((8, QBLK), F32)
        inner = jnp.zeros((8, QBLK), F32)
        peak = None
        for c in range(nc):
            total, inner = weigh(h, c, m, total, inner)
        total = jnp.sum(total, axis=0, keepdims=True)
        inner = jnp.sum(inner, axis=0, keepdims=True)
        inv = 1.0 / total
        inner = inner * inv
        for c in range(nc):
            finish(h, c, inv, inner)
            if h + 1 < heads:
                peak = products(h + 1, c, peak)
    part(heads, reps, rows, ds_ref, p_ref, keys // 2, qbuf, gbuf, far_out)


def part(heads, reps, rows, ds_ref, p_ref, base, qbuf, gbuf, out_ref):
    for r in range(reps):
        at = base + r * rows
        ds = ds_ref[at:at + rows, :]
        p = p_ref[at:at + rows, :]
        kp = lax.dot_general(ds, qbuf[...], NN, preferred_element_type=F32)
        vp = lax.dot_general(p, gbuf[...], NN, preferred_element_type=F32)
        out_ref[:, r * DK:r * DK + DL] = (kp[:, :DL] + vp).astype(BF16)
        out_ref[:, r * DK + DL:(r + 1) * DK] = kp[:, DL:].astype(BF16)


def part_kernel(heads, reps, ds_ref, p_ref, qbuf, gbuf, near_out):
    part(heads, reps, near_out.shape[0], ds_ref, p_ref, 0, qbuf, gbuf, near_out)


def query_kernel(heads, reps, near_ref, far_ref, ds_ref, ready_ref, dq_ref, ktbuf):
    rows = near_ref.shape[0]
    for half, ref in enumerate((near_ref, far_ref)):
        for r in range(reps):
            at = (half * reps + r) * rows
            ktbuf[:, at:at + rows] = ref[:, r * DK:(r + 1) * DK].T
    for h in range(heads):
        dqt = lax.dot_general(ktbuf[...], ds_ref[:, h * QBLK:(h + 1) * QBLK], NN, preferred_element_type=F32)
        dq_ref[:, h * DK:(h + 1) * DK] = dqt.T.astype(BF16)


VM = pl.BlockSpec(memory_space=pltpu.VMEM)


def attend_scores(near, far, q, g):
    rows = near.shape[0]
    reps = near.shape[1] // DK
    heads = q.shape[1] // DK
    keys = 2 * rows * reps
    return pl.pallas_call(
        functools.partial(scores_kernel, heads, reps),
        out_shape=(
            jax.ShapeDtypeStruct((keys, heads * QBLK), BF16),
            jax.ShapeDtypeStruct((keys, heads * QBLK), BF16),
            jax.ShapeDtypeStruct(far.shape, BF16),
            jax.ShapeDtypeStruct((heads * QBLK, DK), BF16),
            jax.ShapeDtypeStruct((heads * QBLK, DL), BF16),
        ),
        in_specs=[VM] * 4,
        out_specs=(VM,) * 5,
        scratch_shapes=[
            pltpu.VMEM((keys, DK), BF16),
            pltpu.VMEM((2, keys, QBLK), F32),
            pltpu.VMEM((2, keys, QBLK), F32),
        ],
        compiler_params=pltpu.CompilerParams(vmem_limit_bytes=30 * 1024 * 1024),
        cost_estimate=pl.CostEstimate(flops=7 * keys * heads * QBLK * DK, bytes_accessed=16 * near.size, transcendentals=keys * heads * QBLK),
        name="attend_scores",
    )(near, far, q, g)


def attend_part(ds, p, qs, gs, shape):
    heads = ds.shape[1] // QBLK
    return pl.pallas_call(
        functools.partial(part_kernel, heads, shape[1] // DK),
        out_shape=jax.ShapeDtypeStruct(shape, BF16),
        in_specs=[VM] * 4,
        out_specs=VM,
        compiler_params=pltpu.CompilerParams(vmem_limit_bytes=20 * 1024 * 1024),
        cost_estimate=pl.CostEstimate(flops=4 * ds.shape[0] // 2 * ds.shape[1] * DK, bytes_accessed=4 * ds.size, transcendentals=0),
        name="attend_part",
    )(ds, p, qs, gs)


def attend_query(near, far, ds, ready):
    heads = ds.shape[1] // QBLK
    reps = near.shape[1] // DK
    return pl.pallas_call(
        functools.partial(query_kernel, heads, reps),
        out_shape=jax.ShapeDtypeStruct((QBLK, heads * DK), BF16),
        in_specs=[VM] * 3 + [pl.BlockSpec(memory_space=pl.ANY)],
        out_specs=VM,
        scratch_shapes=[pltpu.VMEM((DK, ds.shape[0]), BF16)],
        compiler_params=pltpu.CompilerParams(vmem_limit_bytes=20 * 1024 * 1024),
        cost_estimate=pl.CostEstimate(flops=2 * ds.size * DK, bytes_accessed=4 * ds.size, transcendentals=0),
        name="attend_query",
    )(near, far, ds, ready)


def serve_kernel(place, picks_ref, cache_ref, out_ref, sums_ref):
    shards, capacity, width = out_ref.shape
    blocks = cache_ref.shape[0]
    asking = shards // 2
    slots = asking * capacity
    per = picks_ref.shape[1]
    total = asking * per
    rows = [picks_ref[pl.ds(2 * z + place[1], 1), :] for z in range(asking)]
    picks = jnp.concatenate(rows, axis=1)
    mine = (picks // blocks) == place[0]
    within = picks % blocks
    first = lax.broadcasted_iota(jnp.int32, (total, total), 0)
    second = lax.broadcasted_iota(jnp.int32, (total, total), 1)
    before = ((first // per == second // per) & (first < second)).astype(BF16)
    marks = jnp.broadcast_to(mine.astype(F32), (8, total)).astype(BF16)
    rank = lax.dot_general(marks, before, NN, preferred_element_type=F32)[:1].astype(jnp.int32)
    slot = lax.broadcasted_iota(jnp.int32, (slots, total), 0)
    asker = lax.broadcasted_iota(jnp.int32, (slots, total), 1) // per
    spot = jnp.where(mine, rank, capacity)
    left = ((slot // capacity == asker) & (slot % capacity == spot)).astype(BF16)
    block = lax.broadcasted_iota(jnp.int32, (blocks, total), 0)
    right = (block == within).astype(BF16)
    chosen = lax.dot_general(left, right, NT, preferred_element_type=F32).astype(BF16)
    sums_ref[...] = lax.dot_general(right, left, NT, preferred_element_type=F32).astype(BF16)
    served = lax.dot_general(chosen, cache_ref[...], NN, preferred_element_type=F32).astype(BF16)
    for z in range(asking):
        part = served[z * capacity:(z + 1) * capacity]
        out_ref[2 * z] = part[:, :width]
        out_ref[2 * z + 1] = part[:, width:]


def serve(place, picks, cache, groups):
    blocks, whole = cache.shape
    shards, per = picks.shape
    width = whole // groups
    capacity = 2 * per // shards
    return pl.pallas_call(
        serve_kernel,
        out_shape=(
            jax.ShapeDtypeStruct((shards, capacity, width), BF16),
            jax.ShapeDtypeStruct((blocks, shards // 2 * capacity), BF16),
        ),
        grid_spec=pltpu.PrefetchScalarGridSpec(
            num_scalar_prefetch=1,
            grid=(1,),
            in_specs=[
                pl.BlockSpec(picks.shape, lambda i, place: (0, 0)),
                pl.BlockSpec((blocks, 2 * width), lambda i, place: (0, place[2])),
            ],
            out_specs=(
                pl.BlockSpec((shards, capacity, width), lambda i, place: (0, 0, 0)),
                pl.BlockSpec((blocks, shards // 2 * capacity), lambda i, place: (0, 0)),
            ),
        ),
        compiler_params=pltpu.CompilerParams(vmem_limit_bytes=58 * 1024 * 1024),
        name="serve",
    )(place, picks, cache)


def compact_kernel(
    block_count, copies, place, picks_ref, recv_ref, first_ready, second_ready, out_ref, spot_ref
):
    shards, capacity, width = recv_ref.shape
    slots = shards * capacity
    per = picks_ref.shape[1]
    picks = picks_ref[pl.ds(place[3], 1), :]
    holder = picks // block_count
    first = lax.broadcasted_iota(jnp.int32, (per, per), 0)
    second = lax.broadcasted_iota(jnp.int32, (per, per), 1)
    shard = lax.broadcasted_iota(jnp.int32, (shards, per), 0)
    held = shard == holder
    before = (first < second).astype(BF16)
    counts = lax.dot_general(held.astype(BF16), before, NN, preferred_element_type=F32)
    rank = jnp.sum(jnp.where(held, counts, 0.0), axis=0, keepdims=True).astype(jnp.int32)
    slot = lax.broadcasted_iota(jnp.int32, (slots, per), 0)
    spots = (slot == holder * capacity + rank).astype(BF16)
    spot_ref[...] = spots
    recv = jnp.concatenate([recv_ref[c] for c in range(shards)], axis=0)
    picked = lax.dot_general(spots, recv, TN, preferred_element_type=F32).astype(BF16)
    for e in range(copies):
        out_ref[e * per:(e + 1) * per, :] = picked


def compact(place, picks, recv, ready, block_count, copies):
    per = picks.shape[1]
    shards, capacity, width = recv.shape
    vm = pl.BlockSpec(memory_space=pltpu.VMEM)
    return pl.pallas_call(
        functools.partial(compact_kernel, block_count, copies),
        out_shape=(
            jax.ShapeDtypeStruct((copies * per, width), BF16),
            jax.ShapeDtypeStruct((shards * capacity, per), BF16),
        ),
        in_specs=[pl.BlockSpec(memory_space=pltpu.SMEM), vm, vm] + [pl.BlockSpec(memory_space=pl.ANY)] * 2,
        out_specs=(vm, vm),
        compiler_params=pltpu.CompilerParams(vmem_limit_bytes=32 * 1024 * 1024),
        name="compact",
    )(place, picks, recv, *ready)


def pair_kernel(own_ref, other_ref, out_ref):
    out_ref[...] = (own_ref[...].astype(F32) + other_ref[...].astype(F32)).astype(BF16)


def pair_sum(own, other):
    vm = pl.BlockSpec(memory_space=pltpu.VMEM)
    return pl.pallas_call(
        pair_kernel,
        out_shape=jax.ShapeDtypeStruct(own.shape, BF16),
        in_specs=[vm, vm],
        out_specs=vm,
        compiler_params=pltpu.CompilerParams(vmem_limit_bytes=32 * 1024 * 1024),
        name="pair_sum",
    )(own, other)


def fold_kernel(part_ref, spot_ref, held_ref, out_ref, same_ref):
    shards, capacity, width = out_ref.shape
    per = spot_ref.shape[1]
    total = part_ref[:per, :].astype(F32)
    for e in range(1, part_ref.shape[0] // per):
        total += part_ref[e * per:(e + 1) * per, :].astype(F32)
    placed = lax.dot_general(
        spot_ref[...], total.astype(BF16), NN, preferred_element_type=F32
    ).astype(BF16)
    for c in range(shards):
        out_ref[c] = placed[c * capacity:(c + 1) * capacity]


def fold(parts, spots, held, shards):
    width = parts.shape[1]
    vm = pl.BlockSpec(memory_space=pltpu.VMEM)
    return pl.pallas_call(
        fold_kernel,
        out_shape=(
            jax.ShapeDtypeStruct((shards, spots.shape[0] // shards, width), BF16),
            jax.ShapeDtypeStruct(held.shape, held.dtype),
        ),
        in_specs=[vm, vm, pl.BlockSpec(memory_space=pl.ANY)],
        out_specs=(vm, pl.BlockSpec(memory_space=pl.ANY)),
        input_output_aliases={2: 1},
        compiler_params=pltpu.CompilerParams(vmem_limit_bytes=32 * 1024 * 1024),
        name="fold",
    )(parts, spots, held)


def collect_kernel(recv_ref, sums_ref, out_ref):
    shards, capacity, width = recv_ref.shape
    size = out_ref.shape[1]
    for k in range(2):
        recv = jnp.concatenate([recv_ref[2 * z + k] for z in range(shards // 2)], axis=0)
        total = lax.dot_general(sums_ref[...], recv, NN, preferred_element_type=F32).astype(BF16)
        for e in range(out_ref.shape[0]):
            out_ref[e, :, k * width:(k + 1) * width] = total[e * size:(e + 1) * size]


def collect(recv, sums, groups):
    width = recv.shape[2]
    vm = pl.BlockSpec(memory_space=pltpu.VMEM)
    return pl.pallas_call(
        collect_kernel,
        out_shape=jax.ShapeDtypeStruct((groups, sums.shape[0] // groups, 2 * width), BF16),
        in_specs=[vm, vm],
        out_specs=vm,
        compiler_params=pltpu.CompilerParams(vmem_limit_bytes=32 * 1024 * 1024),
        name="collect",
    )(recv, sums)


def settle_kernel(columns, recv_ref, moved_ref, out_ref, query_ref, sem):
    copy = pltpu.make_async_copy(moved_ref, query_ref, sem)
    copy.start()
    width = recv_ref.shape[2]
    for u in range(recv_ref.shape[0] // 2):
        y, half = u // (columns // 2), u % (columns // 2)
        first = y * columns + 2 * half
        both = recv_ref[first].astype(F32) + recv_ref[first + 1].astype(F32)
        out_ref[:, u * width:(u + 1) * width] = both.astype(BF16)
    copy.wait()


def settle(recv, moved, columns):
    groups, rows, width = recv.shape
    vm = pl.BlockSpec(memory_space=pltpu.VMEM)
    hbm = pl.BlockSpec(memory_space=pl.ANY)
    return pl.pallas_call(
        functools.partial(settle_kernel, columns),
        out_shape=(
            jax.ShapeDtypeStruct((rows, groups // 2 * width), BF16),
            jax.ShapeDtypeStruct(moved.shape, BF16),
        ),
        in_specs=[vm, hbm],
        out_specs=(vm, hbm),
        scratch_shapes=[pltpu.SemaphoreType.DMA],
        compiler_params=pltpu.CompilerParams(vmem_limit_bytes=32 * 1024 * 1024),
        name="settle",
    )(recv, moved)


COLUMNS = 4


def colour(group):
    return (group // COLUMNS + group % COLUMNS) % 2


def on_device(queries, latent_cache, block_picks, out_grad):
    shards = lax.axis_size("ctx")
    groups = lax.axis_size("grp")
    block_count = latent_cache.shape[0]
    ctx = lax.axis_index("ctx")
    grp = lax.axis_index("grp")
    mark = colour(grp)
    place = jnp.stack([ctx, mark, grp // 2, ctx // 2 * 2 + mark]).astype(jnp.int32)
    swap = []
    for c in range(shards):
        for e in range(groups):
            moved = c % 2 != colour(e)
            swap.append((c * groups + e, (c ^ 1) * groups + (e ^ 1) if moved else c * groups + e))
    sides = [[e for e in range(groups) if colour(e) == side] for side in range(2)]
    cores = [(c, c ^ 1) for c in range(shards)]
    moved_queries = lax.ppermute(queries, ("ctx", "grp"), swap)
    moved_grad = lax.ppermute(out_grad, ("ctx", "grp"), swap)
    spread = lax.broadcasted_iota(jnp.int32, (shards, block_picks.shape[1]), 0) == ctx
    every = lax.psum(jnp.where(spread, block_picks, 0), "ctx")
    served, sums = serve(place, every, latent_cache, groups)
    fetched = lax.all_to_all(served, "ctx", split_axis=0, concat_axis=0, tiled=True)
    picked, spots = compact(
        place, every, fetched, (moved_queries, moved_grad), block_count, groups // 2
    )
    near = lax.all_to_all(
        picked, "grp", split_axis=0, concat_axis=0, tiled=True, axis_index_groups=sides
    )
    far = lax.ppermute(near, "ctx", cores)
    ds, probs, far_part, query_rows, grad_rows = attend_scores(near, far, moved_queries, moved_grad)
    other_part = lax.ppermute(far_part, "ctx", cores)
    near_part = attend_part(ds, probs, query_rows, grad_rows, near.shape)
    chip_part = pair_sum(near_part, other_part)
    parts = lax.all_to_all(
        chip_part, "grp", split_axis=0, concat_axis=0, tiled=True, axis_index_groups=sides
    )
    part_query_grad = attend_query(near, far, ds, chip_part)
    placed, held_query_grad = fold(parts, spots, part_query_grad, shards)
    moved_query_grad = lax.ppermute(held_query_grad, ("ctx", "grp"), swap)
    returned = lax.all_to_all(placed, "ctx", split_axis=0, concat_axis=0, tiled=True)
    owned = collect(returned, sums, groups)
    final = lax.all_to_all(owned, "grp", split_axis=0, concat_axis=0, tiled=True)
    latent_grad, query_grad = settle(final, moved_query_grad, COLUMNS)
    return (query_grad, latent_grad)


def solution(mesh):
    placed = (P("ctx", "grp"), P("ctx", None), P("ctx", None), P("ctx", "grp"))
    return jax.shard_map(
        on_device,
        mesh=mesh,
        in_specs=placed,
        out_specs=(P("ctx", "grp"), P(("ctx", "grp"), None)),
        check_vma=False,
    )
```

time: 166 us -> 153 us (0.922)
  blocking collectives: 136 us -> 90.1 us
  waiting for transfers between devices: 0 us -> 14.6 us
  starting transfers between devices: 0 us -> 14.3 us
  Pallas kernels: 24.6 us -> 27.1 us
    all_to_all x2 -> x1, blocking collectives: 73.8 us -> 25.2 us  [on_device(): lax.all_to_all(picked, 'grp', split_axis=0, concat_axis=0, tiled=True, ax...]
    unnamed x1 -> x0, blocking collectives: 15.3 us -> none
    psum x0 -> x1, blocking collectives: none -> 14.4 us  [on_device(): every = lax.psum(jnp.where(spread, block_picks, 0), 'ctx')]
    all_to_all x0 -> x1, waiting for transfers between devices: none -> 12.1 us  [on_device(): lax.all_to_all(chip_part, 'grp', split_axis=0, concat_axis=0, tiled=True,...]
    ppermute x0 -> x5, starting transfers between devices: none -> 10.7 us  [the longest x1 4.51 us: on_device(): moved_queries = lax.ppermute(queries, ('ctx', 'grp'), swap)]
    all_to_all x1, blocking collectives: 12.1 us -> 17.4 us  [on_device(): lax.all_to_all(owned, 'grp', split_axis=0, concat_axis=0, tiled=True)]
    all_to_all x0 -> x1, starting transfers between devices: none -> 3.56 us  [on_device(): lax.all_to_all(chip_part, 'grp', split_axis=0, concat_axis=0, tiled=True,...]
    ppermute x0 -> x5, waiting for transfers between devices: none -> 2.48 us  [the longest x1 2.47 us: on_device(): far = lax.ppermute(near, 'ctx', cores)]
  transfers between devices with their start and end apart: 0 -> 6, of which waited for: 0 -> 2; matrix products, arithmetic and copies ran while one was open for 0% -> 1% of each run, Pallas kernels for 0% -> 6%
where the time goes in v2:
time: 153 us; the launch traced here: 152 us
  blocking collectives  90.1 us (59%)
  Pallas kernels  27.1 us (18%)
  waiting for transfers between devices  14.6 us (10%)
  starting transfers between devices  14.3 us (9%)
  local copies, waits for them, and re-layouts  3.47 us (2%)
    all_to_all x1, blocking collectives, on_device(): lax.all_to_all(picked, 'grp', split_axis=0, concat_axis=0, tiled=True, ax...  25.2 us
    all_to_all x1, blocking collectives, on_device(): lax.all_to_all(served, 'ctx', split_axis=0, concat_axis=0, tiled=True)  18.4 us
    all_to_all x1, blocking collectives, on_device(): lax.all_to_all(owned, 'grp', split_axis=0, concat_axis=0, tiled=True)  17.4 us
    all_to_all x1, blocking collectives, on_device(): lax.all_to_all(placed, 'ctx', split_axis=0, concat_axis=0, tiled=True)  14.7 us
    psum x1, blocking collectives, on_device(): every = lax.psum(jnp.where(spread, block_picks, 0), 'ctx')  14.4 us
    pallas_call x1, Pallas kernels, attend_scores(): pl.pallas_call(functools.partial(scores_kernel, heads, reps), out_shape=(...  13.3 us
    all_to_all x1, waiting for transfers between devices, on_device(): lax.all_to_all(chip_part, 'grp', split_axis=0, concat_axis=0, tiled=True,...  12.1 us
    ppermute x1, starting transfers between devices, on_device(): moved_queries = lax.ppermute(queries, ('ctx', 'grp'), swap)  4.51 us
  transfers between devices with their start and end apart: 6, of which 2 were waited for; matrix products, arithmetic and copies ran while one was open for 1% of the time, Pallas kernels for 6%

profile of v2, /device:TPU:1, one launch (start us, length us, event | category | flops | bytes accessed | tf_op | source)
XLA Modules:
  0.0 151.9 jit_solution(6769329791604788623)
XLA Ops:
  0.6 4.5 %collective-permute-start = (bf16[256,2304]{1,0:T(8,128)(2,1)}, bf16[256,2304]{1,0:T(8,128)(2,1)S(1)}, u32[]{:S(2)}, u32[]{:S(2)}) collective-permute-start(bf16[256,2304]{1,0:T(8,128)(2,1)} %param.4), channel_id=1, source_target_pairs={{0,0},{1,16},{2,2},{3,18},{4,21},{5,5},{6,23},{7,7},{8,8},{9,24},{... | collective-permute-start | bytes 3538952 | tf_op jit(solution)/shard_map/ppermute | solution.py:390
  5.1 1.9 %collective-permute-start.1 = (bf16[256,2048]{1,0:T(8,128)(2,1)}, bf16[256,2048]{1,0:T(8,128)(2,1)S(1)}, u32[]{:S(2)}, u32[]{:S(2)}) collective-permute-start(bf16[256,2048]{1,0:T(8,128)(2,1)} %param.7), channel_id=1, source_target_pairs={{0,0},{1,16},{2,2},{3,18},{4,21},{5,5},{6,23},{7,7},{8,8},{9,24},{... | collective-permute-start | bytes 3145736 | tf_op jit(solution)/shard_map/ppermute | solution.py:391
  7.1 0.7 broadcast_select_fusion
  7.9 14.4 %psum.7.picks_ref = s32[16,32]{1,0:T(8,128)} all-reduce(s32[16,32]{1,0:T(8,128)S(1)} %broadcast_select_fusion), channel_id=1, replica_groups=mesh['ctx'=16,'grp'=16] {'ctx'}, use_global_device_ids=true, to_apply=%region_0.1 | all-reduce | flops 512 | bytes 4096 | tf_op jit(solution)/shard_map/psum | solution.py:393
  22.3 0.6 pad_add_fusion.place
  22.9 3.1 %serve.1 = (bf16[16,4,2304]{2,1,0:T(4,128)(2,1)}, bf16[64,32]{1,0:T(8,128)(2,1)}) custom-call(s32[4]{0:T(128)} %pad_add_fusion.place, s32[16,32]{1,0:T(8,128)} %psum.7.picks_ref, bf16[64,36864]{1,0:T(8,128)(2,1)} %cache_ref.1), custom_call_target="tpu_custom_call" | custom-call | tf_op jit(solution)/shard_map/serve/pallas_call | solution.py:205
  26.1 18.4 %all_to_all.37.recv_ref = bf16[16,4,2304]{2,1,0:T(4,128)(2,1)S(1)} all-to-all(bf16[16,4,2304]{2,1,0:T(4,128)(2,1)} %get-tuple-element.15), channel_id=1, replica_groups=mesh['ctx'=16,'grp'=16] {'ctx'}, dimensions={0} | all-to-all | bytes 589824 | tf_op jit(solution)/shard_map/all_to_all | solution.py:395
  44.5 1.0 compact.1
  45.5 25.2 %all_to_all.38 = bf16[8,32,2304]{2,1,0:T(8,128)(2,1)S(1)} all-to-all(bf16[8,32,2304]{2,1,0:T(8,128)(2,1)S(1)} %bitcast.13), channel_id=1, replica_groups={{0,2,5,7,8,10,13,15},{1,3,4,6,9,11,12,14},{16,18,21,23,24,26,29,31},{17..., dimensions={0} | all-to-all | bytes 2359296 | tf_op jit(solution)/shard_map/all_to_all | solution.py:399
  70.6 0.8 collective-permute-start.2
  71.4 2.5 %collective-permute-done.2.far_ref = bf16[256,2304]{1,0:T(8,128)(2,1)S(1)} collective-permute-done((bf16[256,2304]{1,0:T(8,128)(2,1)S(1)}, bf16[256,2304]{1,0:T(8,128)(2,1)S(1)}, u32[]{:S(2)}, u32[]{:S(2)}) %collective-permute-start.2) | collective-permute-done | bytes 1179680 | tf_op jit(solution)/shard_map/ppermute | solution.py:402
  73.9 13.3 %attend_scores.1 = (bf16[2048,1024]{1,0:T(8,128)(2,1)S(1)}, bf16[2048,1024]{1,0:T(8,128)(2,1)S(1)}, bf16[256,2304]{1,0:T(8,128)(2,1)S(1)}, bf16[1024,576]{1,0:T(8,128)(2,1)S(1)}, bf16[1024,512]{1,0:T(8,128)(2,1)S(1)}) custom-call(bf16[256,2304]{1,0:T(8,128)(2,1)S(1)} %bitcast.11, bf16[256,2304]{1,0:T(8,128)(2,1)S(1)} %collective-permute-done.2.far_ref, ...), custom_call_target="tpu_custom_call" | custom-call | flops 8455716864 | bytes 9437184 | tf_op jit(solution)/shard_map/attend_scores/pallas_call | solution.py:119
  87.2 0.6 collective-permute-start.3
  87.8 2.9 %attend_part.1.own_ref = bf16[256,2304]{1,0:T(8,128)(2,1)S(1)} custom-call(bf16[2048,1024]{1,0:T(8,128)(2,1)S(1)} %get-tuple-element.17.ds_ref, bf16[2048,1024]{1,0:T(8,128)(2,1)S(1)} %get-tuple-element.18.p_ref, bf16[1024,576]{1,0:T(8,128)(2,1)S(1)} %get-tuple-element.19.qbuf, bf16[1024,512]{1,0:T(8,128)(2,1)S(1)} %get-tuple-element.20.gbuf), custom_call_target="tpu_custom_call" | custom-call | flops 2415919104 | bytes 8388608 | tf_op jit(solution)/shard_map/attend_part/pallas_call | solution.py:143
  90.8 1.3 pair_sum.1.ready_ref
  92.1 3.6 %all-to-all-start.2 = ((bf16[8,32,2304]{2,1,0:T(8,128)(2,1)}), bf16[8,32,2304]{2,1,0:T(8,128)(2,1)S(1)}, u32[]{:S(2)}, u32[]{:S(2)}) async-start(bf16[8,32,2304]{2,1,0:T(8,128)(2,1)} %bitcast.7), calls=%async_computation.2 | async-start | bytes 2359296 | tf_op jit(solution)/shard_map/all_to_all | solution.py:407
  95.7 2.2 %copy-done.1 = bf16[2048,1024]{1,0:T(8,128)(2,1)S(1)} copy-done((bf16[2048,1024]{1,0:T(8,128)(2,1)S(1)}, bf16[2048,1024]{1,0:T(8,128)(2,1)}, u32[]{:S(2)}) %copy-start.1) | copy-done | bytes 4194328
  97.8 1.3 copy-done.6
  99.1 3.2 %attend_query.1.held_ref = bf16[256,2304]{1,0:T(8,128)(2,1)S(1)} custom-call(bf16[256,2304]{1,0:T(8,128)(2,1)S(1)} %bitcast.12, bf16[256,2304]{1,0:T(8,128)(2,1)S(1)} %copy-done.6, bf16[2048,1024]{1,0:T(8,128)(2,1)S(1)} %copy-done.1, bf16[256,2304]{1,0:T(8,128)(2,1)} %pair_sum.1.ready_ref), custom_call_target="tpu_custom_call" | custom-call | flops 2415919104 | bytes 8388608 | tf_op jit(solution)/shard_map/attend_query/pallas_call | solution.py:157
  102.3 12.1 %all-to-all-done.2 = bf16[8,32,2304]{2,1,0:T(8,128)(2,1)S(1)} async-done(((bf16[8,32,2304]{2,1,0:T(8,128)(2,1)}), bf16[8,32,2304]{2,1,0:T(8,128)(2,1)S(1)}, u32[]{:S(2)}, u32[]{:S(2)}) %all-to-all-start.2) | async-done | bytes 1179680 | tf_op jit(solution)/shard_map/all_to_all | solution.py:407
  114.7 2.8 %collective-permute-start.4 = (bf16[256,2304]{1,0:T(8,128)(2,1)S(1)}, bf16[256,2304]{1,0:T(8,128)(2,1)S(1)}, u32[]{:S(2)}, u32[]{:S(2)}) collective-permute-start(bf16[256,2304]{1,0:T(8,128)(2,1)S(1)} %get-tuple-element.25), channel_id=1, source_target_pairs={{0,0},{1,16},{2,2},{3,18},{4,21},{5,5},{6,23},{7,7},{8,8},{9,24},{... | collective-permute-start | bytes 3538952 | tf_op jit(solution)/shard_map/ppermute | solution.py:412
  117.6 14.7 %all_to_all.39.recv_ref = bf16[16,4,2304]{2,1,0:T(4,128)(2,1)S(1)} all-to-all(bf16[16,4,2304]{2,1,0:T(4,128)(2,1)S(1)} %get-tuple-element.23), channel_id=1, replica_groups=mesh['ctx'=16,'grp'=16] {'ctx'}, dimensions={0} | all-to-all | bytes 589824 | tf_op jit(solution)/shard_map/all_to_all | solution.py:413
  132.6 17.4 %all_to_all.40.recv_ref = bf16[16,4,4608]{2,1,0:T(4,128)(2,1)S(1)} all-to-all(bf16[16,4,4608]{2,1,0:T(4,128)(2,1)S(1)} %collect.1), channel_id=1, replica_groups=mesh['ctx'=16,'grp'=16] {'grp'}, dimensions={0} | all-to-all | bytes 1179648 | tf_op jit(solution)/shard_map/all_to_all | solution.py:415
  150.0 1.7 %settle.1 = (bf16[4,36864]{1,0:T(4,128)(2,1)}, bf16[256,2304]{1,0:T(8,128)(2,1)}) custom-call(bf16[16,4,4608]{2,1,0:T(4,128)(2,1)S(1)} %all_to_all.40.recv_ref, bf16[256,2304]{1,0:T(8,128)(2,1)S(1)} %collective-permute-done.4.moved_ref), custom_call_target="tpu_custom_call" | custom-call | tf_op jit(solution)/shard_map/settle/pallas_call | solution.py:354
  (19 shorter events, 0.7 us)
Async XLA Ops:
  0.6 43.8 %collective-permute-start = (bf16[256,2304]{1,0:T(8,128)(2,1)}, bf16[256,2304]{1,0:T(8,128)(2,1)S(1)}, u32[]{:S(2)}, u32[]{:S(2)}) collective-permute-start(bf16[256,2304]{1,0:T(8,128)(2,1)} %param.4), channel_id=1, source_target_pairs={{0,0},{1,16},{2,2},{3,18},{4,21},{5,5},{6,23},{7,7},{8,8},{9,24},{... | collective-permute-start | bytes 3538952 | tf_op jit(solution)/shard_map/ppermute | solution.py:390
  5.1 39.3 %collective-permute-start.1 = (bf16[256,2048]{1,0:T(8,128)(2,1)}, bf16[256,2048]{1,0:T(8,128)(2,1)S(1)}, u32[]{:S(2)}, u32[]{:S(2)}) collective-permute-start(bf16[256,2048]{1,0:T(8,128)(2,1)} %param.7), channel_id=1, source_target_pairs={{0,0},{1,16},{2,2},{3,18},{4,21},{5,5},{6,23},{7,7},{8,8},{9,24},{... | collective-permute-start | bytes 3145736 | tf_op jit(solution)/shard_map/ppermute | solution.py:391
  22.9 21.5 %copy-start.2 = (s32[16,32]{1,0:T(8,128)S(1)}, s32[16,32]{1,0:T(8,128)}, u32[]{:S(2)}) copy-start(s32[16,32]{1,0:T(8,128)} %psum.7.picks_ref) | copy-start | bytes 6148
  22.9 21.5 %copy-start.4 = (s32[4]{0:T(128)S(1)}, s32[4]{0:T(128)}, u32[]{:S(2)}) copy-start(s32[4]{0:T(128)} %pad_add_fusion.place) | copy-start | bytes 52
  70.6 3.3 %collective-permute-start.2 = (bf16[256,2304]{1,0:T(8,128)(2,1)S(1)}, bf16[256,2304]{1,0:T(8,128)(2,1)S(1)}, u32[]{:S(2)}, u32[]{:S(2)}) collective-permute-start(bf16[256,2304]{1,0:T(8,128)(2,1)S(1)} %bitcast.10), channel_id=1, source_target_pairs={{0,16},{16,0},{32,48},{48,32},{64,80},{80,64},{96,112},{112,96},{1... | collective-permute-start | bytes 3538952 | tf_op jit(solution)/shard_map/ppermute | solution.py:402
  73.9 13.3 %copy-start.5 = (bf16[256,2304]{1,0:T(8,128)(2,1)}, bf16[256,2304]{1,0:T(8,128)(2,1)S(1)}, u32[]{:S(2)}) copy-start(bf16[256,2304]{1,0:T(8,128)(2,1)S(1)} %collective-permute-done.2.far_ref) | copy-start | bytes 3538948
  87.2 3.6 %copy-start = (bf16[2048,1024]{1,0:T(8,128)(2,1)}, bf16[2048,1024]{1,0:T(8,128)(2,1)S(1)}, u32[]{:S(2)}) copy-start(bf16[2048,1024]{1,0:T(8,128)(2,1)S(1)} %get-tuple-element.17.ds_ref) | copy-start | bytes 12582916
  87.2 3.6 %collective-permute-start.3 = (bf16[256,2304]{1,0:T(8,128)(2,1)S(1)}, bf16[256,2304]{1,0:T(8,128)(2,1)S(1)}, u32[]{:S(2)}, u32[]{:S(2)}) collective-permute-start(bf16[256,2304]{1,0:T(8,128)(2,1)S(1)} %get-tuple-element.21), channel_id=1, source_target_pairs={{0,16},{16,0},{32,48},{48,32},{64,80},{80,64},{96,112},{112,96},{1... | collective-permute-start | bytes 3538952 | tf_op jit(solution)/shard_map/ppermute | solution.py:404
  92.1 22.3 %all-to-all-start.2 = ((bf16[8,32,2304]{2,1,0:T(8,128)(2,1)}), bf16[8,32,2304]{2,1,0:T(8,128)(2,1)S(1)}, u32[]{:S(2)}, u32[]{:S(2)}) async-start(bf16[8,32,2304]{2,1,0:T(8,128)(2,1)} %bitcast.7), calls=%async_computation.2 | async-start | bytes 2359296 | tf_op jit(solution)/shard_map/all_to_all | solution.py:407
  95.6 2.2 %copy-start.1 = (bf16[2048,1024]{1,0:T(8,128)(2,1)S(1)}, bf16[2048,1024]{1,0:T(8,128)(2,1)}, u32[]{:S(2)}) copy-start(bf16[2048,1024]{1,0:T(8,128)(2,1)} %copy-done) | copy-start | bytes 12582916
  97.8 1.3 copy-start.6
  114.4 17.9 %copy-start.3 = (bf16[64,32]{1,0:T(8,128)(2,1)S(1)}, bf16[64,32]{1,0:T(8,128)(2,1)}, u32[]{:S(2)}) copy-start(bf16[64,32]{1,0:T(8,128)(2,1)} %get-tuple-element.24.sums_ref) | copy-start | bytes 12292
  114.7 35.3 %collective-permute-start.4 = (bf16[256,2304]{1,0:T(8,128)(2,1)S(1)}, bf16[256,2304]{1,0:T(8,128)(2,1)S(1)}, u32[]{:S(2)}, u32[]{:S(2)}) collective-permute-start(bf16[256,2304]{1,0:T(8,128)(2,1)S(1)} %get-tuple-element.25), channel_id=1, source_target_pairs={{0,0},{1,16},{2,2},{3,18},{4,21},{5,5},{6,23},{7,7},{8,8},{9,24},{... | collective-permute-start | bytes 3538952 | tf_op jit(solution)/shard_map/ppermute | solution.py:412

commit v3 on v2

v3 whole, which is shorter than its diff:
```python
import functools
import jax
import jax.numpy as jnp
from jax import lax
from jax.experimental import pallas as pl
from jax.experimental.pallas import tpu as pltpu
from jax.sharding import PartitionSpec as P

DL = 512
DR = 64
QBLK = 256
DK = 576
SCORE_SCALE = 192.0 ** (-0.5)
LOG2E = 1.4426950408889634
F32 = jnp.float32
BF16 = jnp.bfloat16
NT = (((1,), (1,)), ((), ()))
NN = (((1,), (0,)), ((), ()))
TN = (((0,), (0,)), ((), ()))


def near_kernel(heads, reps, near_ref, q_ref, g_ref, s_ref, dp_ref, peak_ref, qbuf, gbuf, kbuf):
    rows = near_ref.shape[0]
    for r in range(reps):
        kbuf[r * rows:(r + 1) * rows, :] = near_ref[:, r * DK:(r + 1) * DK]
    for h in range(heads):
        qbuf[h * QBLK:(h + 1) * QBLK, :] = q_ref[:, h * DK:(h + 1) * DK]
        gbuf[h * QBLK:(h + 1) * QBLK, :] = g_ref[:, h * DL:(h + 1) * DL]
    for h in range(heads):
        at = slice(h * QBLK, (h + 1) * QBLK)
        s = lax.dot_general(kbuf[...], qbuf[at, :], NT, preferred_element_type=F32)
        s_ref[:, at] = s
        dp_ref[:, at] = lax.dot_general(
            kbuf[:, :DL], gbuf[at, :], NT, preferred_element_type=F32
        )
        peak_ref[:, at] = jnp.max(s.reshape(s.shape[0] // 8, 8, QBLK), axis=0)


def scores_kernel(heads, reps, far_ref, s_ref, dp_ref, peak_ref, qbuf, gbuf, ds_ref, p_ref, far_out,
                  kbuf, sbuf, dpbuf, wbuf, pbuf):
    rows = far_ref.shape[0]
    keys = rows * reps
    for r in range(reps):
        kbuf[r * rows:(r + 1) * rows, :] = far_ref[:, r * DK:(r + 1) * DK]
    kc = 256
    nc = keys // kc
    factor = SCORE_SCALE * LOG2E

    def products(h, c, peak):
        at = slice(h * QBLK, (h + 1) * QBLK)
        to = slice(c * kc, (c + 1) * kc)
        s = lax.dot_general(kbuf[to, :], qbuf[at, :], NT, preferred_element_type=F32)
        sbuf[h % 2, to, :] = s
        dpbuf[h % 2, to, :] = lax.dot_general(
            kbuf[to, :DL], gbuf[at, :], NT, preferred_element_type=F32
        )
        return jnp.maximum(peak, jnp.max(s.reshape(kc // 8, 8, QBLK), axis=0))

    def held(h, c):
        at = slice(h * QBLK, (h + 1) * QBLK)
        if c < nc:
            to = slice(c * kc, (c + 1) * kc)
            return s_ref[to, at], dp_ref[to, at]
        to = slice((c - nc) * kc, (c - nc + 1) * kc)
        return sbuf[h % 2, to, :], dpbuf[h % 2, to, :]

    def peak_of(h):
        return peak_ref[:, h * QBLK:(h + 1) * QBLK]

    peak = peak_of(0)
    for c in range(nc):
        peak = products(0, c, peak)
    for h in range(heads):
        at = slice(h * QBLK, (h + 1) * QBLK)
        m = jnp.max(peak, axis=0, keepdims=True)
        total = jnp.zeros((8, QBLK), F32)
        inner = jnp.zeros((8, QBLK), F32)
        for c in range(2 * nc):
            s, dp = held(h, c)
            w = jnp.exp2((s - m) * factor)
            wbuf[c * kc:(c + 1) * kc, :] = w
            total += jnp.sum(w.reshape(kc // 8, 8, QBLK), axis=0)
            inner += jnp.sum((w * dp).reshape(kc // 8, 8, QBLK), axis=0)
        inv = 1.0 / jnp.sum(total, axis=0, keepdims=True)
        inner = jnp.sum(inner, axis=0, keepdims=True) * inv
        if h + 1 < heads:
            peak = peak_of(h + 1)
        for c in range(2 * nc):
            dp = held(h, c)[1]
            a = wbuf[c * kc:(c + 1) * kc, :] * inv
            d = a * ((dp - inner) * SCORE_SCALE)
            if c < nc:
                p_ref[c * kc:(c + 1) * kc, at] = a.astype(BF16)
            else:
                pbuf[(c - nc) * kc:(c - nc + 1) * kc, at] = a.astype(BF16)
            ds_ref[c * kc:(c + 1) * kc, at] = d.astype(BF16)
            if h + 1 < heads and c % 2 == 1:
                peak = products(h + 1, c // 2, peak)
    part(heads, reps, rows, ds_ref, keys, pbuf, qbuf, gbuf, far_out)


def part(heads, reps, rows, ds_ref, base, p_ref, qbuf, gbuf, out_ref):
    for r in range(reps):
        ds = ds_ref[base + r * rows:base + (r + 1) * rows, :]
        p = p_ref[r * rows:(r + 1) * rows, :]
        kp = lax.dot_general(ds, qbuf[...], NN, preferred_element_type=F32)
        vp = lax.dot_general(p, gbuf[...], NN, preferred_element_type=F32)
        out_ref[:, r * DK:r * DK + DL] = (kp[:, :DL] + vp).astype(BF16)
        out_ref[:, r * DK + DL:(r + 1) * DK] = kp[:, DL:].astype(BF16)


def part_kernel(heads, reps, ds_ref, p_ref, qbuf, gbuf, near_out):
    part(heads, reps, near_out.shape[0], ds_ref, 0, p_ref, qbuf, gbuf, near_out)


def query_kernel(heads, reps, near_ref, far_ref, ds_ref, ready_ref, dq_ref, ktbuf):
    rows = near_ref.shape[0]
    for half, ref in enumerate((near_ref, far_ref)):
        for r in range(reps):
            at = (half * reps + r) * rows
            ktbuf[:, at:at + rows] = ref[:, r * DK:(r + 1) * DK].T
    for h in range(heads):
        dqt = lax.dot_general(ktbuf[...], ds_ref[:, h * QBLK:(h + 1) * QBLK], NN, preferred_element_type=F32)
        dq_ref[:, h * DK:(h + 1) * DK] = dqt.T.astype(BF16)


VM = pl.BlockSpec(memory_space=pltpu.VMEM)


def attend_near(near, q, g):
    rows = near.shape[0]
    reps = near.shape[1] // DK
    heads = q.shape[1] // DK
    keys = rows * reps
    wide = heads * QBLK
    return pl.pallas_call(
        functools.partial(near_kernel, heads, reps),
        out_shape=(
            jax.ShapeDtypeStruct((keys, wide), F32),
            jax.ShapeDtypeStruct((keys, wide), F32),
            jax.ShapeDtypeStruct((8, wide), F32),
            jax.ShapeDtypeStruct((wide, DK), BF16),
            jax.ShapeDtypeStruct((wide, DL), BF16),
        ),
        in_specs=[VM] * 3,
        out_specs=(VM,) * 5,
        scratch_shapes=[pltpu.VMEM((keys, DK), BF16)],
        compiler_params=pltpu.CompilerParams(vmem_limit_bytes=20 * 1024 * 1024),
        cost_estimate=pl.CostEstimate(
            flops=4 * keys * wide * DK, bytes_accessed=16 * near.size, transcendentals=0
        ),
        name="attend_near",
    )(near, q, g)


def attend_scores(far, scores, dprobs, peaks, qs, gs):
    rows = far.shape[0]
    reps = far.shape[1] // DK
    heads = qs.shape[0] // QBLK
    keys = rows * reps
    wide = heads * QBLK
    return pl.pallas_call(
        functools.partial(scores_kernel, heads, reps),
        out_shape=(
            jax.ShapeDtypeStruct((2 * keys, wide), BF16),
            jax.ShapeDtypeStruct((keys, wide), BF16),
            jax.ShapeDtypeStruct(far.shape, BF16),
        ),
        in_specs=[VM] * 6,
        out_specs=(VM,) * 3,
        scratch_shapes=[
            pltpu.VMEM((keys, DK), BF16),
            pltpu.VMEM((2, keys, QBLK), F32),
            pltpu.VMEM((2, keys, QBLK), F32),
            pltpu.VMEM((2 * keys, QBLK), F32),
            pltpu.VMEM((keys, wide), BF16),
        ],
        compiler_params=pltpu.CompilerParams(vmem_limit_bytes=34 * 1024 * 1024),
        cost_estimate=pl.CostEstimate(
            flops=6 * keys * wide * DK, bytes_accessed=16 * far.size, transcendentals=keys * wide
        ),
        name="attend_scores",
    )(far, scores, dprobs, peaks, qs, gs)


def attend_part(ds, p, qs, gs, shape):
    heads = ds.shape[1] // QBLK
    return pl.pallas_call(
        functools.partial(part_kernel, heads, shape[1] // DK),
        out_shape=jax.ShapeDtypeStruct(shape, BF16),
        in_specs=[VM] * 4,
        out_specs=VM,
        compiler_params=pltpu.CompilerParams(vmem_limit_bytes=16 * 1024 * 1024),
        cost_estimate=pl.CostEstimate(flops=4 * ds.shape[0] // 2 * ds.shape[1] * DK, bytes_accessed=4 * ds.size, transcendentals=0),
        name="attend_part",
    )(ds, p, qs, gs)


def attend_query(near, far, ds, ready):
    heads = ds.shape[1] // QBLK
    reps = near.shape[1] // DK
    return pl.pallas_call(
        functools.partial(query_kernel, heads, reps),
        out_shape=jax.ShapeDtypeStruct((QBLK, heads * DK), BF16),
        in_specs=[VM] * 3 + [pl.BlockSpec(memory_space=pl.ANY)],
        out_specs=VM,
        scratch_shapes=[pltpu.VMEM((DK, ds.shape[0]), BF16)],
        compiler_params=pltpu.CompilerParams(vmem_limit_bytes=14 * 1024 * 1024),
        cost_estimate=pl.CostEstimate(flops=2 * ds.size * DK, bytes_accessed=4 * ds.size, transcendentals=0),
        name="attend_query",
    )(near, far, ds, ready)


def serve_kernel(picks_ref, cache_ref, out_ref, sums_ref, slice_ref, sem):
    shards, capacity, width = out_ref.shape
    blocks = cache_ref.shape[0]
    me = lax.axis_index("ctx")
    group = lax.axis_index("grp")
    start = pl.multiple_of((group // 2) * (2 * width), 128)
    copy = pltpu.make_async_copy(cache_ref.at[:, pl.ds(start, 2 * width)], slice_ref, sem)
    copy.start()
    asking = shards // 2
    slots = asking * capacity
    per = picks_ref.shape[1]
    total = asking * per
    mark = colour(group)
    rows = [picks_ref[pl.ds(2 * z + mark, 1), :] for z in range(asking)]
    picks = jnp.concatenate(rows, axis=1)
    mine = (picks // blocks) == me
    within = picks % blocks
    first = lax.broadcasted_iota(jnp.int32, (total, total), 0)
    second = lax.broadcasted_iota(jnp.int32, (total, total), 1)
    before = ((first // per == second // per) & (first < second)).astype(BF16)
    marks = jnp.broadcast_to(mine.astype(F32), (8, total)).astype(BF16)
    rank = lax.dot_general(marks, before, NN, preferred_element_type=F32)[:1].astype(jnp.int32)
    slot = lax.broadcasted_iota(jnp.int32, (slots, total), 0)
    asker = lax.broadcasted_iota(jnp.int32, (slots, total), 1) // per
    spot = jnp.where(mine, rank, capacity)
    left = ((slot // capacity == asker) & (slot % capacity == spot)).astype(BF16)
    block = lax.broadcasted_iota(jnp.int32, (blocks, total), 0)
    right = (block == within).astype(BF16)
    chosen = lax.dot_general(left, right, NT, preferred_element_type=F32).astype(BF16)
    sums_ref[...] = lax.dot_general(right, left, NT, preferred_element_type=F32).astype(BF16)
    copy.wait()
    served = lax.dot_general(chosen, slice_ref[...], NN, preferred_element_type=F32).astype(BF16)
    for z in range(asking):
        part = served[z * capacity:(z + 1) * capacity]
        out_ref[2 * z] = part[:, :width]
        out_ref[2 * z + 1] = part[:, width:]


def serve(picks, cache, groups):
    blocks, whole = cache.shape
    shards, per = picks.shape
    width = whole // groups
    capacity = 2 * per // shards
    return pl.pallas_call(
        serve_kernel,
        out_shape=(
            jax.ShapeDtypeStruct((shards, capacity, width), BF16),
            jax.ShapeDtypeStruct((blocks, shards // 2 * capacity), BF16),
        ),
        in_specs=[VM, pl.BlockSpec(memory_space=pl.ANY)],
        out_specs=(VM, VM),
        scratch_shapes=[pltpu.VMEM((blocks, 2 * width), BF16), pltpu.SemaphoreType.DMA],
        compiler_params=pltpu.CompilerParams(vmem_limit_bytes=58 * 1024 * 1024),
        name="serve",
    )(picks, cache)


def compact_kernel(
    block_count, copies, picks_ref, recv_ref, first_ready, second_ready, out_ref, spot_ref
):
    shards, capacity, width = recv_ref.shape
    slots = shards * capacity
    per = picks_ref.shape[1]
    row = lax.axis_index("ctx") // 2 * 2 + colour(lax.axis_index("grp"))
    picks = picks_ref[pl.ds(row, 1), :]
    holder = picks // block_count
    first = lax.broadcasted_iota(jnp.int32, (per, per), 0)
    second = lax.broadcasted_iota(jnp.int32, (per, per), 1)
    shard = lax.broadcasted_iota(jnp.int32, (shards, per), 0)
    held = shard == holder
    before = (first < second).astype(BF16)
    counts = lax.dot_general(held.astype(BF16), before, NN, preferred_element_type=F32)
    rank = jnp.sum(jnp.where(held, counts, 0.0), axis=0, keepdims=True).astype(jnp.int32)
    slot = lax.broadcasted_iota(jnp.int32, (slots, per), 0)
    spots = (slot == holder * capacity + rank).astype(BF16)
    spot_ref[...] = spots
    recv = jnp.concatenate([recv_ref[c] for c in range(shards)], axis=0)
    picked = lax.dot_general(spots, recv, TN, preferred_element_type=F32).astype(BF16)
    for e in range(copies):
        out_ref[e * per:(e + 1) * per, :] = picked


def compact(picks, recv, ready, block_count, copies):
    per = picks.shape[1]
    shards, capacity, width = recv.shape
    vm = pl.BlockSpec(memory_space=pltpu.VMEM)
    return pl.pallas_call(
        functools.partial(compact_kernel, block_count, copies),
        out_shape=(
            jax.ShapeDtypeStruct((copies * per, width), BF16),
            jax.ShapeDtypeStruct((shards * capacity, per), BF16),
        ),
        in_specs=[vm, vm] + [pl.BlockSpec(memory_space=pl.ANY)] * 2,
        out_specs=(vm, vm),
        compiler_params=pltpu.CompilerParams(vmem_limit_bytes=8 * 1024 * 1024),
        name="compact",
    )(picks, recv, *ready)


def pair_kernel(own_ref, other_ref, out_ref):
    out_ref[...] = (own_ref[...].astype(F32) + other_ref[...].astype(F32)).astype(BF16)


def pair_sum(own, other):
    vm = pl.BlockSpec(memory_space=pltpu.VMEM)
    return pl.pallas_call(
        pair_kernel,
        out_shape=jax.ShapeDtypeStruct(own.shape, BF16),
        in_specs=[vm, vm],
        out_specs=vm,
        compiler_params=pltpu.CompilerParams(vmem_limit_bytes=8 * 1024 * 1024),
        name="pair_sum",
    )(own, other)


def fold_kernel(part_ref, spot_ref, out_ref):
    shards, capacity, width = out_ref.shape
    per = spot_ref.shape[1]
    total = part_ref[:per, :].astype(F32)
    for e in range(1, part_ref.shape[0] // per):
        total += part_ref[e * per:(e + 1) * per, :].astype(F32)
    placed = lax.dot_general(
        spot_ref[...], total.astype(BF16), NN, preferred_element_type=F32
    ).astype(BF16)
    for c in range(shards):
        out_ref[c] = placed[c * capacity:(c + 1) * capacity]


def fold(parts, spots, shards):
    width = parts.shape[1]
    vm = pl.BlockSpec(memory_space=pltpu.VMEM)
    return pl.pallas_call(
        fold_kernel,
        out_shape=jax.ShapeDtypeStruct((shards, spots.shape[0] // shards, width), BF16),
        in_specs=[vm, vm],
        out_specs=vm,
        compiler_params=pltpu.CompilerParams(vmem_limit_bytes=8 * 1024 * 1024),
        name="fold",
    )(parts, spots)


def collect_kernel(recv_ref, sums_ref, out_ref):
    shards, capacity, width = recv_ref.shape
    size = out_ref.shape[1]
    for k in range(2):
        recv = jnp.concatenate([recv_ref[2 * z + k] for z in range(shards // 2)], axis=0)
        total = lax.dot_general(sums_ref[...], recv, NN, preferred_element_type=F32).astype(BF16)
        for e in range(out_ref.shape[0]):
            out_ref[e, :, k * width:(k + 1) * width] = total[e * size:(e + 1) * size]


def collect(recv, sums, groups):
    width = recv.shape[2]
    vm = pl.BlockSpec(memory_space=pltpu.VMEM)
    return pl.pallas_call(
        collect_kernel,
        out_shape=jax.ShapeDtypeStruct((groups, sums.shape[0] // groups, 2 * width), BF16),
        in_specs=[vm, vm],
        out_specs=vm,
        compiler_params=pltpu.CompilerParams(vmem_limit_bytes=8 * 1024 * 1024),
        name="collect",
    )(recv, sums)


def settle_kernel(columns, recv_ref, moved_ref, out_ref, query_ref, sem):
    copy = pltpu.make_async_copy(moved_ref, query_ref, sem)
    copy.start()
    width = recv_ref.shape[2]
    for u in range(recv_ref.shape[0] // 2):
        y, half = u // (columns // 2), u % (columns // 2)
        first = y * columns + 2 * half
        both = recv_ref[first].astype(F32) + recv_ref[first + 1].astype(F32)
        out_ref[:, u * width:(u + 1) * width] = both.astype(BF16)
    copy.wait()


def settle(recv, moved, columns):
    groups, rows, width = recv.shape
    vm = pl.BlockSpec(memory_space=pltpu.VMEM)
    hbm = pl.BlockSpec(memory_space=pl.ANY)
    return pl.pallas_call(
        functools.partial(settle_kernel, columns),
        out_shape=(
            jax.ShapeDtypeStruct((rows, groups // 2 * width), BF16),
            jax.ShapeDtypeStruct(moved.shape, BF16),
        ),
        in_specs=[vm, hbm],
        out_specs=(vm, hbm),
        scratch_shapes=[pltpu.SemaphoreType.DMA],
        compiler_params=pltpu.CompilerParams(vmem_limit_bytes=8 * 1024 * 1024),
        name="settle",
    )(recv, moved)


COLUMNS = 4


def colour(group):
    return (group // COLUMNS + group % COLUMNS) % 2


def on_device(queries, latent_cache, block_picks, out_grad):
    shards = lax.axis_size("ctx")
    groups = lax.axis_size("grp")
    block_count = latent_cache.shape[0]
    ctx = lax.axis_index("ctx")
    swap = []
    for c in range(shards):
        for e in range(groups):
            moved = c % 2 != colour(e)
            swap.append((c * groups + e, (c ^ 1) * groups + (e ^ 1) if moved else c * groups + e))
    sides = [[e for e in range(groups) if colour(e) == side] for side in range(2)]
    cores = [(c, c ^ 1) for c in range(shards)]
    moved_queries = lax.ppermute(queries, ("ctx", "grp"), swap)
    moved_grad = lax.ppermute(out_grad, ("ctx", "grp"), swap)
    spread = lax.broadcasted_iota(jnp.int32, (shards, block_picks.shape[1]), 0) == ctx
    every = lax.psum(jnp.where(spread, block_picks, 0), "ctx")
    served, sums = serve(every, latent_cache, groups)
    fetched = lax.all_to_all(served, "ctx", split_axis=0, concat_axis=0, tiled=True)
    picked, spots = compact(
        every, fetched, (moved_queries, moved_grad), block_count, groups // 2
    )
    near = lax.all_to_all(
        picked, "grp", split_axis=0, concat_axis=0, tiled=True, axis_index_groups=sides
    )
    far = lax.ppermute(near, "ctx", cores)
    scores, dprobs, peaks, query_rows, grad_rows = attend_near(near, moved_queries, moved_grad)
    ds, probs, far_part = attend_scores(far, scores, dprobs, peaks, query_rows, grad_rows)
    other_part = lax.ppermute(far_part, "ctx", cores)
    near_part = attend_part(ds, probs, query_rows, grad_rows, near.shape)
    chip_part = pair_sum(near_part, other_part)
    parts = lax.all_to_all(
        chip_part, "grp", split_axis=0, concat_axis=0, tiled=True, axis_index_groups=sides
    )
    part_query_grad = attend_query(near, far, ds, chip_part)
    moved_query_grad = lax.ppermute(part_query_grad, ("ctx", "grp"), swap)
    placed = fold(parts, spots, shards)
    returned = lax.all_to_all(placed, "ctx", split_axis=0, concat_axis=0, tiled=True)
    owned = collect(returned, sums, groups)
    final = lax.all_to_all(owned, "grp", split_axis=0, concat_axis=0, tiled=True)
    latent_grad, query_grad = settle(final, moved_query_grad, COLUMNS)
    return (query_grad, latent_grad)


def solution(mesh):
    placed = (P("ctx", "grp"), P("ctx", None), P("ctx", None), P("ctx", "grp"))
    return jax.shard_map(
        on_device,
        mesh=mesh,
        in_specs=placed,
        out_specs=(P("ctx", "grp"), P(("ctx", "grp"), None)),
        check_vma=False,
    )
```

time: 153 us -> 148 us (0.967)
  blocking collectives: 90.1 us -> 73.4 us
  waiting for transfers between devices: 14.6 us -> 20.8 us
  starting transfers between devices: 14.3 us -> 18.6 us
  Pallas kernels: 27.1 us -> 29.2 us
    all_to_all x1 -> x0, blocking collectives: 17.4 us -> none  [on_device(): lax.all_to_all(owned, 'grp', split_axis=0, concat_axis=0, tiled=True)]
    all_to_all x0 -> x1, waiting for transfers between devices: none -> 13.1 us  [on_device(): lax.all_to_all(owned, 'grp', split_axis=0, concat_axis=0, tiled=True)]
    all_to_all x0 -> x1, starting transfers between devices: none -> 4.44 us  [on_device(): lax.all_to_all(owned, 'grp', split_axis=0, concat_axis=0, tiled=True)]
    all_to_all x1, waiting for transfers between devices: 12.1 us -> 7.72 us  [on_device(): lax.all_to_all(chip_part, 'grp', split_axis=0, concat_axis=0, tiled=True,...]
    pallas_call x1 -> x2, Pallas kernels: 0.33 us -> 3.27 us  [the longest x1 2.94 us: attend_near(): pl.pallas_call(functools.partial(near_kernel, heads, reps), out_shape=(ja...]
    ppermute x1, waiting for transfers between devices: 2.47 us -> 0.01 us  [on_device(): far = lax.ppermute(near, 'ctx', cores)]
    pallas_call x1, Pallas kernels: 13.3 us -> 11.3 us  [attend_scores(): pl.pallas_call(functools.partial(scores_kernel, heads, reps), out_shape=(...]
    unnamed x14 -> x12, local copies, waits for them, and re-layouts: 3.47 us -> 3.47 us
  transfers between devices with their start and end apart: 6 -> 7, of which waited for: 2 -> 2; matrix products, arithmetic and copies ran while one was open for 1% -> 0% of each run, Pallas kernels for 6% -> 10%
where the time goes in v3:
time: 148 us; the launch traced here: 147 us
  blocking collectives  73.4 us (50%)
  Pallas kernels  29.2 us (20%)
  waiting for transfers between devices  20.8 us (14%)
  starting transfers between devices  18.6 us (13%)
  local copies, waits for them, and re-layouts  3.47 us (2%)
    all_to_all x1, blocking collectives, on_device(): lax.all_to_all(picked, 'grp', split_axis=0, concat_axis=0, tiled=True, ax...  25.2 us
    all_to_all x1, blocking collectives, on_device(): lax.all_to_all(served, 'ctx', split_axis=0, concat_axis=0, tiled=True)  18.4 us
    all_to_all x1, blocking collectives, on_device(): lax.all_to_all(placed, 'ctx', split_axis=0, concat_axis=0, tiled=True)  15.4 us
    psum x1, blocking collectives, on_device(): every = lax.psum(jnp.where(spread, block_picks, 0), 'ctx')  14.4 us
    all_to_all x1, waiting for transfers between devices, on_device(): lax.all_to_all(owned, 'grp', split_axis=0, concat_axis=0, tiled=True)  13.1 us
    pallas_call x1, Pallas kernels, attend_scores(): pl.pallas_call(functools.partial(scores_kernel, heads, reps), out_shape=(...  11.3 us
    all_to_all x1, waiting for transfers between devices, on_device(): lax.all_to_all(chip_part, 'grp', split_axis=0, concat_axis=0, tiled=True,...  7.72 us
    ppermute x1, starting transfers between devices, on_device(): moved_queries = lax.ppermute(queries, ('ctx', 'grp'), swap)  4.51 us
  transfers between devices with their start and end apart: 7, of which 2 were waited for; matrix products, arithmetic and copies ran while one was open for 0% of the time, Pallas kernels for 10%

profile of v3, /device:TPU:1, one launch (start us, length us, event | category | flops | bytes accessed | tf_op | source)
XLA Modules:
  0.0 147.1 jit_solution(7392011162627523074)
XLA Ops:
  0.6 4.5 %collective-permute-start = (bf16[256,2304]{1,0:T(8,128)(2,1)}, bf16[256,2304]{1,0:T(8,128)(2,1)S(1)}, u32[]{:S(2)}, u32[]{:S(2)}) collective-permute-start(bf16[256,2304]{1,0:T(8,128)(2,1)} %param.4), channel_id=1, source_target_pairs={{0,0},{1,16},{2,2},{3,18},{4,21},{5,5},{6,23},{7,7},{8,8},{9,24},{... | collective-permute-start | bytes 3538952 | tf_op jit(solution)/shard_map/ppermute | solution.py:427
  5.1 1.9 %collective-permute-start.1 = (bf16[256,2048]{1,0:T(8,128)(2,1)}, bf16[256,2048]{1,0:T(8,128)(2,1)S(1)}, u32[]{:S(2)}, u32[]{:S(2)}) collective-permute-start(bf16[256,2048]{1,0:T(8,128)(2,1)} %param.7), channel_id=1, source_target_pairs={{0,0},{1,16},{2,2},{3,18},{4,21},{5,5},{6,23},{7,7},{8,8},{9,24},{... | collective-permute-start | bytes 3145736 | tf_op jit(solution)/shard_map/ppermute | solution.py:428
  7.1 0.7 broadcast_select_fusion
  7.8 14.4 %psum.7.picks_ref = s32[16,32]{1,0:T(8,128)} all-reduce(s32[16,32]{1,0:T(8,128)S(1)} %broadcast_select_fusion), channel_id=1, replica_groups=mesh['ctx'=16,'grp'=16] {'ctx'}, use_global_device_ids=true, to_apply=%region_0.1 | all-reduce | flops 512 | bytes 4096 | tf_op jit(solution)/shard_map/psum | solution.py:430
  22.3 2.8 %serve.1 = (bf16[16,4,2304]{2,1,0:T(4,128)(2,1)}, bf16[64,32]{1,0:T(8,128)(2,1)}) custom-call(s32[16,32]{1,0:T(8,128)} %psum.7.picks_ref, bf16[64,36864]{1,0:T(8,128)(2,1)} %cache_ref.1), custom_call_target="tpu_custom_call" | custom-call | tf_op jit(solution)/shard_map/serve/pallas_call | solution.py:257
  25.1 18.4 %all_to_all.37.recv_ref = bf16[16,4,2304]{2,1,0:T(4,128)(2,1)S(1)} all-to-all(bf16[16,4,2304]{2,1,0:T(4,128)(2,1)} %get-tuple-element.16), channel_id=1, replica_groups=mesh['ctx'=16,'grp'=16] {'ctx'}, dimensions={0} | all-to-all | bytes 589824 | tf_op jit(solution)/shard_map/all_to_all | solution.py:432
  43.5 0.4 compact.1
  44.0 25.2 %all_to_all.38 = bf16[8,32,2304]{2,1,0:T(8,128)(2,1)S(1)} all-to-all(bf16[8,32,2304]{2,1,0:T(8,128)(2,1)S(1)} %bitcast.9), channel_id=1, replica_groups={{0,2,5,7,8,10,13,15},{1,3,4,6,9,11,12,14},{16,18,21,23,24,26,29,31},{17..., dimensions={0} | all-to-all | bytes 2359296 | tf_op jit(solution)/shard_map/all_to_all | solution.py:436
  69.1 0.8 collective-permute-start.2
  69.9 2.9 %attend_near.1 = (f32[1024,1024]{1,0:T(8,128)S(1)}, f32[1024,1024]{1,0:T(8,128)S(1)}, f32[8,1024]{1,0:T(8,128)S(1)}, bf16[1024,576]{1,0:T(8,128)(2,1)S(1)}, bf16[1024,512]{1,0:T(8,128)(2,1)S(1)}) custom-call(bf16[256,2304]{1,0:T(8,128)(2,1)S(1)} %bitcast.7, bf16[256,2304]{1,0:T(8,128)(2,1)S(1)} %collective-permute-done.first_ready.q_ref, ...), custom_call_target="tpu_custom_call" | custom-call | flops 2415919104 | bytes 9437184 | tf_op jit(solution)/shard_map/attend_near/pallas_call | solution.py:136
  72.9 11.3 %attend_scores.1 = (bf16[2048,1024]{1,0:T(8,128)(2,1)S(1)}, bf16[1024,1024]{1,0:T(8,128)(2,1)S(1)}, bf16[256,2304]{1,0:T(8,128)(2,1)S(1)}) custom-call(bf16[256,2304]{1,0:T(8,128)(2,1)S(1)} %collective-permute-done.2.far_ref, f32[1024,1024]{1,0:T(8,128)S(1)} %get-tuple-element.18.s_ref, f32[1024,1024]{1,0:T(8,128)S(1)} %get-tuple-element.19.dp_ref, ...), custom_call_target="tpu_custom_call" | custom-call | flops 3623878656 | bytes 9437184 | tf_op jit(solution)/shard_map/attend_scores/pallas_call | solution.py:162
  84.3 2.9 %attend_part.1.own_ref = bf16[256,2304]{1,0:T(8,128)(2,1)S(1)} custom-call(bf16[2048,1024]{1,0:T(8,128)(2,1)S(1)} %get-tuple-element.23.ds_ref, bf16[1024,1024]{1,0:T(8,128)(2,1)S(1)} %get-tuple-element.24.p_ref, bf16[1024,576]{1,0:T(8,128)(2,1)S(1)} %get-tuple-element.21.qbuf, bf16[1024,512]{1,0:T(8,128)(2,1)S(1)} %get-tuple-element.22.gbuf), custom_call_target="tpu_custom_call" | custom-call | flops 2415919104 | bytes 8388608 | tf_op jit(solution)/shard_map/attend_part/pallas_call | solution.py:188
  87.3 1.3 pair_sum.1.ready_ref
  88.6 3.6 %all-to-all-start.2 = ((bf16[8,32,2304]{2,1,0:T(8,128)(2,1)}), bf16[8,32,2304]{2,1,0:T(8,128)(2,1)S(1)}, u32[]{:S(2)}, u32[]{:S(2)}) async-start(bf16[8,32,2304]{2,1,0:T(8,128)(2,1)} %bitcast.3), calls=%async_computation.2 | async-start | bytes 2359296 | tf_op jit(solution)/shard_map/all_to_all | solution.py:445
  92.2 2.2 %copy-done.1 = bf16[2048,1024]{1,0:T(8,128)(2,1)S(1)} copy-done((bf16[2048,1024]{1,0:T(8,128)(2,1)S(1)}, bf16[2048,1024]{1,0:T(8,128)(2,1)}, u32[]{:S(2)}) %copy-start.1) | copy-done | bytes 4194328
  94.4 1.3 copy-done.5
  95.6 4.2 %attend_query.1 = bf16[256,2304]{1,0:T(8,128)(2,1)} custom-call(bf16[256,2304]{1,0:T(8,128)(2,1)S(1)} %bitcast.8, bf16[256,2304]{1,0:T(8,128)(2,1)S(1)} %copy-done.5, bf16[2048,1024]{1,0:T(8,128)(2,1)S(1)} %copy-done.1, bf16[256,2304]{1,0:T(8,128)(2,1)} %pair_sum.1.ready_ref), custom_call_target="tpu_custom_call" | custom-call | flops 2415919104 | bytes 8388608 | tf_op jit(solution)/shard_map/attend_query/pallas_call | solution.py:202
  99.9 3.3 %collective-permute-start.4 = (bf16[256,2304]{1,0:T(8,128)(2,1)}, bf16[256,2304]{1,0:T(8,128)(2,1)S(1)}, u32[]{:S(2)}, u32[]{:S(2)}) collective-permute-start(bf16[256,2304]{1,0:T(8,128)(2,1)} %attend_query.1), channel_id=1, source_target_pairs={{0,0},{1,16},{2,2},{3,18},{4,21},{5,5},{6,23},{7,7},{8,8},{9,24},{... | collective-permute-start | bytes 3538952 | tf_op jit(solution)/shard_map/ppermute | solution.py:449
  103.1 7.7 %all-to-all-done.2 = bf16[8,32,2304]{2,1,0:T(8,128)(2,1)S(1)} async-done(((bf16[8,32,2304]{2,1,0:T(8,128)(2,1)}), bf16[8,32,2304]{2,1,0:T(8,128)(2,1)S(1)}, u32[]{:S(2)}, u32[]{:S(2)}) %all-to-all-start.2) | async-done | bytes 1179680 | tf_op jit(solution)/shard_map/all_to_all | solution.py:445
  111.2 15.4 %all_to_all.39.recv_ref = bf16[16,4,2304]{2,1,0:T(4,128)(2,1)S(1)} all-to-all(bf16[16,4,2304]{2,1,0:T(4,128)(2,1)S(1)} %fold.1), channel_id=1, replica_groups=mesh['ctx'=16,'grp'=16] {'ctx'}, dimensions={0} | all-to-all | bytes 589824 | tf_op jit(solution)/shard_map/all_to_all | solution.py:451
  126.6 1.1 collect.1
  127.7 4.4 %all-to-all-start.4 = ((bf16[16,4,4608]{2,1,0:T(4,128)(2,1)}), bf16[16,4,4608]{2,1,0:T(4,128)(2,1)S(1)}, u32[]{:S(2)}, u32[]{:S(2)}) async-start(bf16[16,4,4608]{2,1,0:T(4,128)(2,1)} %collect.1), calls=%async_computation.4 | async-start | bytes 1179648 | tf_op jit(solution)/shard_map/all_to_all | solution.py:453
  132.2 13.1 %all-to-all-done.4.recv_ref = bf16[16,4,4608]{2,1,0:T(4,128)(2,1)S(1)} async-done(((bf16[16,4,4608]{2,1,0:T(4,128)(2,1)}), bf16[16,4,4608]{2,1,0:T(4,128)(2,1)S(1)}, u32[]{:S(2)}, u32[]{:S(2)}) %all-to-all-start.4) | async-done | bytes 589856 | tf_op jit(solution)/shard_map/all_to_all | solution.py:453
  145.2 1.7 %settle.1 = (bf16[4,36864]{1,0:T(4,128)(2,1)}, bf16[256,2304]{1,0:T(8,128)(2,1)}) custom-call(bf16[16,4,4608]{2,1,0:T(4,128)(2,1)S(1)} %all-to-all-done.4.recv_ref, bf16[256,2304]{1,0:T(8,128)(2,1)S(1)} %collective-permute-done.4.moved_ref), custom_call_target="tpu_custom_call" | custom-call | tf_op jit(solution)/shard_map/settle/pallas_call | solution.py:394
  (18 shorter events, 0.5 us)
Async XLA Ops:
  0.6 42.9 %collective-permute-start = (bf16[256,2304]{1,0:T(8,128)(2,1)}, bf16[256,2304]{1,0:T(8,128)(2,1)S(1)}, u32[]{:S(2)}, u32[]{:S(2)}) collective-permute-start(bf16[256,2304]{1,0:T(8,128)(2,1)} %param.4), channel_id=1, source_target_pairs={{0,0},{1,16},{2,2},{3,18},{4,21},{5,5},{6,23},{7,7},{8,8},{9,24},{... | collective-permute-start | bytes 3538952 | tf_op jit(solution)/shard_map/ppermute | solution.py:427
  5.1 38.4 %collective-permute-start.1 = (bf16[256,2048]{1,0:T(8,128)(2,1)}, bf16[256,2048]{1,0:T(8,128)(2,1)S(1)}, u32[]{:S(2)}, u32[]{:S(2)}) collective-permute-start(bf16[256,2048]{1,0:T(8,128)(2,1)} %param.7), channel_id=1, source_target_pairs={{0,0},{1,16},{2,2},{3,18},{4,21},{5,5},{6,23},{7,7},{8,8},{9,24},{... | collective-permute-start | bytes 3145736 | tf_op jit(solution)/shard_map/ppermute | solution.py:428
  22.3 21.2 %copy-start.2 = (s32[16,32]{1,0:T(8,128)S(1)}, s32[16,32]{1,0:T(8,128)}, u32[]{:S(2)}) copy-start(s32[16,32]{1,0:T(8,128)} %psum.7.picks_ref) | copy-start | bytes 6148
  69.1 3.8 %collective-permute-start.2 = (bf16[256,2304]{1,0:T(8,128)(2,1)S(1)}, bf16[256,2304]{1,0:T(8,128)(2,1)S(1)}, u32[]{:S(2)}, u32[]{:S(2)}) collective-permute-start(bf16[256,2304]{1,0:T(8,128)(2,1)S(1)} %bitcast.6), channel_id=1, source_target_pairs={{0,16},{16,0},{32,48},{48,32},{64,80},{80,64},{96,112},{112,96},{1... | collective-permute-start | bytes 3538952 | tf_op jit(solution)/shard_map/ppermute | solution.py:439
  72.9 11.3 %copy-start.4 = (bf16[256,2304]{1,0:T(8,128)(2,1)}, bf16[256,2304]{1,0:T(8,128)(2,1)S(1)}, u32[]{:S(2)}) copy-start(bf16[256,2304]{1,0:T(8,128)(2,1)S(1)} %collective-permute-done.2.far_ref) | copy-start | bytes 3538948
  84.2 3.1 %copy-start = (bf16[2048,1024]{1,0:T(8,128)(2,1)}, bf16[2048,1024]{1,0:T(8,128)(2,1)S(1)}, u32[]{:S(2)}) copy-start(bf16[2048,1024]{1,0:T(8,128)(2,1)S(1)} %get-tuple-element.23.ds_ref) | copy-start | bytes 12582916
  84.2 3.1 %collective-permute-start.3 = (bf16[256,2304]{1,0:T(8,128)(2,1)S(1)}, bf16[256,2304]{1,0:T(8,128)(2,1)S(1)}, u32[]{:S(2)}, u32[]{:S(2)}) collective-permute-start(bf16[256,2304]{1,0:T(8,128)(2,1)S(1)} %get-tuple-element.25), channel_id=1, source_target_pairs={{0,16},{16,0},{32,48},{48,32},{64,80},{80,64},{96,112},{112,96},{1... | collective-permute-start | bytes 3538952 | tf_op jit(solution)/shard_map/ppermute | solution.py:442
  88.6 22.3 %all-to-all-start.2 = ((bf16[8,32,2304]{2,1,0:T(8,128)(2,1)}), bf16[8,32,2304]{2,1,0:T(8,128)(2,1)S(1)}, u32[]{:S(2)}, u32[]{:S(2)}) async-start(bf16[8,32,2304]{2,1,0:T(8,128)(2,1)} %bitcast.3), calls=%async_computation.2 | async-start | bytes 2359296 | tf_op jit(solution)/shard_map/all_to_all | solution.py:445
  92.2 2.2 %copy-start.1 = (bf16[2048,1024]{1,0:T(8,128)(2,1)S(1)}, bf16[2048,1024]{1,0:T(8,128)(2,1)}, u32[]{:S(2)}) copy-start(bf16[2048,1024]{1,0:T(8,128)(2,1)} %copy-done) | copy-start | bytes 12582916
  94.4 1.3 copy-start.5
  99.9 26.7 %copy-start.3 = (bf16[64,32]{1,0:T(8,128)(2,1)S(1)}, bf16[64,32]{1,0:T(8,128)(2,1)}, u32[]{:S(2)}) copy-start(bf16[64,32]{1,0:T(8,128)(2,1)} %get-tuple-element.27.sums_ref) | copy-start | bytes 12292
  99.9 32.3 %collective-permute-start.4 = (bf16[256,2304]{1,0:T(8,128)(2,1)}, bf16[256,2304]{1,0:T(8,128)(2,1)S(1)}, u32[]{:S(2)}, u32[]{:S(2)}) collective-permute-start(bf16[256,2304]{1,0:T(8,128)(2,1)} %attend_query.1), channel_id=1, source_target_pairs={{0,0},{1,16},{2,2},{3,18},{4,21},{5,5},{6,23},{7,7},{8,8},{9,24},{... | collective-permute-start | bytes 3538952 | tf_op jit(solution)/shard_map/ppermute | solution.py:449
  127.7 17.5 %all-to-all-start.4 = ((bf16[16,4,4608]{2,1,0:T(4,128)(2,1)}), bf16[16,4,4608]{2,1,0:T(4,128)(2,1)S(1)}, u32[]{:S(2)}, u32[]{:S(2)}) async-start(bf16[16,4,4608]{2,1,0:T(4,128)(2,1)} %collect.1), calls=%async_computation.4 | async-start | bytes 1179648 | tf_op jit(solution)/shard_map/all_to_all | solution.py:453
